TPU v7x, 32 devices: a whole 2x2x4 slice. The times are simulated.
32 devices in a mesh: grp: 4 (over x, core), sub: 8 (over z, y).
Axes of the slice: x: 2, y: 2, z: 4, core: 2. Of those that a mesh axis runs over, the one named last changes fastest.
Arguments:
- operators: float32 [4, 8, 4, 512, 512], P('grp', 'sub'), may hold values from -1 to 6
- counts: int32 [4, 8], P('grp', 'sub'), may hold values from 1 to 4, as said below
- pair_rows: int32 [4, 8, 4, 256], P('grp', 'sub'), may hold values from -256 to 256, as said below
- gap: float32 [4, 8, 4, 256, 128], P('grp', 'sub'), may hold values from -6 to 6
Outputs:
- multipliers: float32 [4, 8, 4, 256, 128], P('grp', 'sub')
- residual: float32 [4, 8, 4, 256, 128], P('grp', 'sub')
Inputs may be any that keep to these rules, and one draw needn't show every extreme that they name: `counts`: each group has at least one owner with 4 subdomains. `pair_rows`: for each group, owner and slot the absolute values are a permutation of 1 to 256.
All inputs are finite; a program needn't handle non-finite values.
Results may differ from a plain program's by a relative error of at most 0.00022.
Values sent between devices are 32-bit elements; how exact they have to be, the bound alone decides.
No kernel may reach another device: no remote copies, remote signals or barrier semaphores. Data moves between devices by JAX's collectives and lax.ppermute only.
A program may use at most 64 MiB of HBM per device.

v0:
```python
import functools

import jax
import jax.numpy as jnp
from jax import lax
from jax.experimental import pallas as pl
from jax.experimental.pallas import tpu as pltpu
from jax.sharding import PartitionSpec as P

ITERS = 6
LOWER = 1.0
UPPER = 14.0
CENTRE = (UPPER + LOWER) / 2.0
RADIUS = (UPPER - LOWER) / 2.0
BF16 = jnp.bfloat16
F32 = jnp.float32
PARTS = 2
VMEM_BYTES = 24 * 1024 * 1024
FIRST_VMEM_BYTES = 51 * 1024 * 1024


def chebyshev_factors():
    spread = CENTRE / RADIUS
    rho = 1.0 / spread
    factors = []
    for _ in range(ITERS - 1):
        rho_new = 1.0 / (2.0 * spread - rho)
        factors.append((rho_new * rho, 2.0 * rho_new / RADIUS))
        rho = rho_new
    return factors


def pairings(groups, owners):
    found = []
    for first in (0, 1):
        route = []
        for g in range(groups):
            for s in range(owners):
                t = s + 1 if (s - first) % 2 == 0 else s - 1
                h = g
                if t < 0 or t >= owners:
                    t = s
                    h = g ^ 1
                if h < groups:
                    route.append((g * owners + s, h * owners + t))
        found.append(route)
    return found


def halves(x):
    high = x.astype(BF16)
    return high, (x - high.astype(F32)).astype(BF16)


def operand(x):
    high, low = halves(x)
    return jnp.concatenate([high, low], axis=0), high


def split_dot(cases, matrix):
    both, high = cases
    h = matrix.shape[0] // 2
    tall = jnp.dot(both, matrix[:h], preferred_element_type=F32)
    rows = high.shape[0]
    return tall[:rows] + tall[rows:] + jnp.dot(high, matrix[h:], preferred_element_type=F32)


def dot_nt(a, b):
    return lax.dot_general(a, b, (((1,), (1,)), ((), ())), preferred_element_type=F32)


def signed_placement(pairs):
    h = pairs.shape[1]
    rows = lax.broadcasted_iota(jnp.int32, (h, h), 0)
    picked = jnp.abs(pairs) - 1
    sign = jnp.where(pairs > 0, 1.0, -1.0)
    return jnp.where(rows == picked, sign, 0.0).astype(BF16)


def row(marks, k):
    return marks[k, pl.ds(0, 1), :]


def mark_places(slots):
    return dict(even=slots, alone=slots + 1, evens=slots + 2, odds=slots + 3)


def first_kernel(owners, counts, operators, pairs, gap, residual, direction, ends, beside_even, beside_odd, marks, pairs_out, source, sems):
    slots = source.shape[0]
    copies = [
        pltpu.make_async_copy(gap.at[0, 0], source, sems.at[0]),
        pltpu.make_async_copy(pairs.at[0, 0], pairs_out, sems.at[1]),
    ]
    for copy in copies:
        copy.start()
    pos = lax.axis_index("sub")
    count = counts[0, 0]
    is_even = lax.rem(pos, 2) == 0
    place = mark_places(slots)
    has_left, has_right = pos > 0, pos < owners - 1
    flags = [count - 1 == j for j in range(slots)] + [None] * 4
    flags[place["even"]] = is_even
    flags[place["alone"]] = count == 1
    flags[place["evens"]] = jnp.logical_or(jnp.logical_and(is_even, has_right), jnp.logical_and(~is_even, has_left))
    flags[place["odds"]] = jnp.logical_or(jnp.logical_and(is_even, has_left), jnp.logical_and(~is_even, has_right))
    for k, flag in enumerate(flags):
        marks[k] = jnp.full(marks.shape[1:], jnp.where(flag, 1.0, 0.0), F32)
    copies[0].wait()
    ends[...] = source[count - 1].T * jnp.where(has_right, 1.0, 0.0)
    for j in range(slots - 1):
        residual[j] = source[j].T * jnp.where(j < count - 1, 1.0, 0.0)
        direction[j] = residual[j] / CENTRE
    put_beside(marks, slots, [direction[j] for j in range(slots - 1)], beside_even, beside_odd)
    copies[1].wait()


def put_beside(marks, slots, blocks, beside_even, beside_odd):
    is_even = row(marks, mark_places(slots)["even"]) > 0.5
    first, before_last = blocks[0], sum(row(marks, j + 1) * blocks[j] for j in range(slots - 1))
    beside_even[...] = jnp.where(is_even, before_last, first)
    beside_odd[...] = jnp.where(is_even, first, before_last)


def operator_kernel(counts, operators, pairs, own_out, lower_out, upper_out, even_out, odd_out):
    slots, h = pairs.shape
    count = counts[0, 0]
    is_even = lax.rem(lax.axis_index("sub"), 2) == 0
    unit = signed_placement(lax.broadcasted_iota(jnp.int32, (1, h), 1) + 1)
    for j in range(slots):
        place = signed_placement(pairs[pl.ds(j, 1), :])
        between = jnp.where(j < count - 1, 1.0, 0.0)
        squares, diagonal, lowers, uppers = [], [], [], []
        for part in halves(operators[0, 0, j]):
            placed = jnp.dot(place, part[:h], preferred_element_type=F32).astype(BF16)
            uppers.append(-dot_nt(unit, placed[:, h:]).astype(BF16))
            lowers.append(-dot_nt(place, part[h:, :h]))
            squares.append(dot_nt(place, placed[:, :h]))
            diagonal.append(dot_nt(unit, part[h:, h:]))
        for k in range(2):
            rows = pl.ds(k * h, h)
            if j < slots - 1:
                lower_out[j, rows, :] = (lowers[k] * between).astype(BF16)
            if j > 0:
                upper_out[j - 1, rows, :] = uppers[k]

            def put_end(out, square, other, rows=rows, k=k):
                out[0, rows, :] = square[k].astype(BF16)
                out[1, rows, :] = other[k].astype(BF16)

            if j == 0:
                pl.when(is_even)(functools.partial(put_end, odd_out, squares, uppers))
                pl.when(~is_even)(functools.partial(put_end, even_out, squares, uppers))
            is_last = count - 1 == j
            pl.when(jnp.logical_and(is_last, is_even))(functools.partial(put_end, even_out, diagonal, lowers))
            pl.when(jnp.logical_and(is_last, ~is_even))(functools.partial(put_end, odd_out, diagonal, lowers))
        if j > 0:
            summed = (previous + (squares[0] + squares[1])) * jnp.where(j < count, 1.0, 0.0)
            own_out[j - 1, pl.ds(0, h), :], own_out[j - 1, pl.ds(h, h), :] = halves(summed)
        previous = diagonal[0] + diagonal[1]


def give(marks, slots, even, odd, beside_even, beside_odd, even_operator, odd_operator):
    alone = row(marks, mark_places(slots)["alone"]) > 0.5
    next_even, next_odd = jnp.where(alone, odd, beside_even), jnp.where(alone, even, beside_odd)
    return (
        split_dot(operand(even), even_operator[0]) + split_dot(operand(next_even), even_operator[1]),
        split_dot(operand(odd), odd_operator[0]) + split_dot(operand(next_odd), odd_operator[1]),
    )


def first_edge_kernel(slots, parts, even_operator, odd_operator, marks, ends, before, beside_even, beside_odd, *outs):
    place = mark_places(slots)
    is_even = row(marks, place["even"]) > 0.5
    even = jnp.where(is_even, ends[...], before[...]) * row(marks, place["evens"])
    odd = jnp.where(is_even, before[...], ends[...]) * row(marks, place["odds"])
    directions = even / CENTRE, odd / CENTRE
    given = give(marks, slots, *directions, beside_even[...], beside_odd[...], even_operator, odd_operator)
    height = even.shape[0] // parts
    for k in range(parts):
        for n, x in enumerate((even, odd, *directions, *given)):
            outs[6 * k + n][...] = x[k * height : (k + 1) * height]


def edge_kernel(factors, slots, start, ends, even_operator, odd_operator, marks, beside_even, beside_odd, *refs):
    even_r, odd_r, even_v, odd_v, even_sent, odd_sent, even_in, odd_in = (ref[...] for ref in refs[:8])
    outs = refs[8:]
    place = mark_places(slots)
    rows = pl.ds(start, even_r.shape[0])
    even_r = (even_r - (even_sent + even_in)) * row(marks, place["evens"])
    odd_r = (odd_r - (odd_sent + odd_in)) * row(marks, place["odds"])
    even_v = factors[0] * even_v + factors[1] * even_r
    odd_v = factors[0] * odd_v + factors[1] * odd_r
    given = give(marks, slots, even_v, odd_v, beside_even[rows, :], beside_odd[rows, :], even_operator, odd_operator)
    if ends:
        is_even = row(marks, place["even"]) > 0.5
        last_r, last_given = jnp.where(is_even, even_r, odd_r), jnp.where(is_even, given[0], given[1])
        results = last_r, last_given, even_v, odd_v, jnp.where(is_even, given[1], given[0])
    else:
        results = even_r, odd_r, even_v, odd_v, *given
    for out, x in zip(outs, results):
        out[...] = x


def inner_kernel(factors, parts, own, lower, upper, marks, direction, residual, *rest):
    rest = list(rest)
    inner = residual.shape[0]
    slots = inner + 1
    even = jnp.concatenate([ref[...] for ref in rest[:parts]], axis=0)
    odd = jnp.concatenate([ref[...] for ref in rest[parts : 2 * parts]], axis=0)
    total, *outs = rest[2 * parts :]
    is_even = row(marks, mark_places(slots)["even"]) > 0.5
    last, before = jnp.where(is_even, even, odd), jnp.where(is_even, odd, even)
    blocks = [row(marks, j) * last + (direction[j] if j < inner else 0.0) for j in range(slots)]
    cases = [operand(block) for block in blocks]
    residual_out, total_out = outs[:2]
    for j in range(slots):
        summed = total[j] + blocks[j]
        total_out[j] = summed if factors is not None else summed.T
    nexts = []
    for j in range(inner):
        image = split_dot(cases[j], own[j]) + split_dot(cases[j + 1], upper[j])
        image += split_dot(cases[j - 1] if j > 0 else operand(before), lower[j])
        left_over = residual[j] - image
        if factors is None:
            residual_out[j] = left_over.T
            continue
        residual_out[j] = left_over
        nexts.append(factors[0] * direction[j] + factors[1] * left_over)
        outs[2][j] = nexts[j]
    if factors is not None:
        put_beside(marks, slots, nexts, outs[3], outs[4])


def last_kernel(parts, marks, residual, *refs):
    out, ready, sems = refs[3 * parts :]
    inner = residual.shape[0]
    slots = inner + 1
    place = mark_places(slots)
    last_r, last_given, came = (
        jnp.concatenate([ref[...] for ref in refs[n * parts : (n + 1) * parts]], axis=0) for n in range(3)
    )
    is_even = row(marks, place["even"]) > 0.5
    shared = jnp.where(is_even, row(marks, place["evens"]), row(marks, place["odds"]))
    last = ((last_r - (last_given + came)) * shared).T
    copies = []
    for j in range(slots):
        mine = marks[j, pl.ds(0, 1), pl.ds(0, last.shape[1])] * last
        ready[j] = mine + residual[j] if j < inner else mine
        copies.append(pltpu.make_async_copy(ready.at[j], out.at[0, 0, j], sems.at[j]))
        copies[j].start()
    for copy in copies:
        copy.wait()


VMEM = pl.BlockSpec(memory_space=pltpu.VMEM)
SMEM = pl.BlockSpec(memory_space=pltpu.SMEM)
HBM = pl.BlockSpec(memory_space=pltpu.HBM)


def in_hbm(x):
    return pltpu.with_memory_space_constraint(x, pltpu.HBM)


def call(kernel, name, ins, outs, scratch=(), out_space=VMEM, vmem=VMEM_BYTES):
    return pl.pallas_call(
        kernel,
        in_specs=ins,
        out_specs=[out_space] * len(outs),
        out_shape=[jax.ShapeDtypeStruct(shape, kind) for shape, kind in outs],
        scratch_shapes=list(scratch),
        compiler_params=pltpu.CompilerParams(vmem_limit_bytes=vmem),
        name=name,
    )


def shards(groups, owners, operators, counts, pair_rows, gap):
    slots, h, cases = gap.shape[2:]
    width = cases // PARTS
    evens, odds = pairings(groups, owners)
    forward = [(s, (s + 1) % owners) for s in range(owners)]
    backward = [(t, s) for s, t in forward]
    field = ((slots, cases, h), F32)
    inner = ((slots - 1, cases, h), F32)
    block = ((cases, h), F32)
    part = ((width, h), F32)
    matrices = ((slots - 1, 2 * h, h), BF16)
    pair = ((2, 2 * h, h), BF16)

    def exchange(even, odd):
        odd = lax.ppermute(odd, ("grp", "sub"), odds)
        even = lax.ppermute(even, ("grp", "sub"), evens)
        return even, odd

    residual, direction, ends, *beside, marks, pairs = call(
        functools.partial(first_kernel, owners),
        "first_blocks",
        [SMEM, HBM, HBM, HBM],
        [inner, inner, block, block, block, ((slots + 4, 8, h), F32), ((slots, h), jnp.int32)],
        [pltpu.VMEM((slots, h, cases), F32), pltpu.SemaphoreType.DMA((2,))],
        vmem=FIRST_VMEM_BYTES,
    )(counts, operators, in_hbm(pair_rows), in_hbm(gap))
    before = lax.ppermute(ends, "sub", forward)
    own, lower, upper, even_operator, odd_operator = call(
        operator_kernel,
        "block_operators",
        [SMEM, VMEM, VMEM],
        [matrices] * 3 + [pair] * 2,
    )(counts, operators, pairs)
    got = call(
        functools.partial(first_edge_kernel, slots, PARTS), "first_edges", [VMEM] * 7, [part] * (6 * PARTS)
    )(even_operator, odd_operator, marks, ends, before, *beside)
    states = [got[6 * k : 6 * k + 6] for k in range(PARTS)]
    total = jnp.zeros(field[0], F32)
    for step, factors in enumerate(chebyshev_factors() + [None]):
        if factors is None:
            came = [lax.ppermute(state[4], "sub", backward) for state in states]
        else:
            came = [exchange(state[4], state[5]) for state in states]
        outs = [inner, field, inner, block, block]
        if factors is None:
            outs = [((slots - 1, h, cases), F32), ((slots, h, cases), F32)]
        got = call(
            functools.partial(inner_kernel, factors, PARTS), "inner_blocks", [VMEM] * (7 + 2 * PARTS), outs
        )(own, lower, upper, marks, direction, residual, *(s[2] for s in states), *(s[3] for s in states), total)
        residual, total = got[:2]
        if factors is not None:
            direction, *beside = got[2:]
            states = [
                call(
                    functools.partial(edge_kernel, factors, slots, k * width, step == ITERS - 2),
                    "edge_blocks",
                    [VMEM] * 13,
                    [part] * (5 if step == ITERS - 2 else 6),
                )(even_operator, odd_operator, marks, *beside, *states[k], *came[k])
                for k in range(PARTS)
            ]
    (residual,) = call(
        functools.partial(last_kernel, PARTS),
        "last_residual",
        [VMEM] * (2 + 3 * PARTS),
        [(gap.shape, F32)],
        [pltpu.VMEM((slots, h, cases), F32), pltpu.SemaphoreType.DMA((slots,))],
        HBM,
    )(marks, residual, *(s[n] for n in (0, 1) for s in states), *came)
    return total[None, None], residual


def solution(mesh):
    groups, owners = mesh.shape["grp"], mesh.shape["sub"]
    return jax.shard_map(
        functools.partial(shards, groups, owners),
        mesh=mesh,
        in_specs=(
            P("grp", "sub", None, None, None),
            P("grp", "sub"),
            P("grp", "sub", None, None),
            P("grp", "sub", None, None, None),
        ),
        out_specs=(P("grp", "sub", None, None, None), P("grp", "sub", None, None, None)),
        check_vma=False,
    )
```

profile of v0, /device:TPU:0, one launch (start us, length us, event | category | flops | bytes accessed | tf_op | source)
XLA Modules:
  0.0 53.5 jit_solution(11104401463391349203)
XLA Ops:
  1.4 1.4 %first_blocks.1 = (f32[3,128,256]{2,1,0:T(8,128)S(1)}, f32[3,128,256]{2,1,0:T(8,128)S(1)}, f32[128,256]{1,0:T(8,128)S(1)}, f32[128,256]{1,0:T(8,128)S(1)}, f32[1...) custom-call(s32[1,1]{1,0:T(1,128)S(6)} %copy.6.counts, f32[1,1,4,512,512]{4,3,2,1,0:T(8,128)} %operators.3, ...), custom_call_target="tpu_custom_call" | custom-call | tf_op jit(solution)/shard_map/first_blocks/pallas_call | solution.py:294
  2.9 3.0 %collective-permute-start = (f32[128,256]{1,0:T(8,128)S(1)}, f32[128,256]{1,0:T(8,128)S(1)}, u32[]{:S(2)}, u32[]{:S(2)}) collective-permute-start(f32[128,256]{1,0:T(8,128)S(1)} %get-tuple-element.120.ends), channel_id=1, source_target_pairs={{0,1},{1,2},{2,3},{3,4},{4,5},{5,6},{6,7},{7,0},{8,9},{9,10},{10,1... | collective-permute-start | bytes 393224 | tf_op jit(solution)/shard_map/ppermute | solution.py:302
  5.9 3.7 %block_operators.1 = (bf16[3,512,256]{2,1,0:T(8,128)(2,1)S(1)}, bf16[3,512,256]{2,1,0:T(8,128)(2,1)S(1)}, bf16[3,512,256]{2,1,0:T(8,128)(2,1)S(1)}, bf16[2,512,2...) custom-call(s32[1,1]{1,0:T(1,128)S(6)} %copy.6.counts, f32[1,1,4,512,512]{4,3,2,1,0:T(8,128)S(1)} %copy-done, ...), custom_call_target="tpu_custom_call" | custom-call | tf_op jit(solution)/shard_map/block_operators/pallas_call | solution.py:303
  9.6 2.9 %collective-permute-done.before = f32[128,256]{1,0:T(8,128)S(1)} collective-permute-done((f32[128,256]{1,0:T(8,128)S(1)}, f32[128,256]{1,0:T(8,128)S(1)}, u32[]{:S(2)}, u32[]{:S(2)}) %collective-permute-start) | collective-permute-done | bytes 131104 | tf_op jit(solution)/shard_map/ppermute | solution.py:302
  12.4 0.4 first_edges.1
  12.9 0.1 collective-permute-start.3
  12.9 0.1 collective-permute-start.4
  13.0 1.9 %collective-permute-start.1 = (f32[64,256]{1,0:T(8,128)S(1)}, f32[64,256]{1,0:T(8,128)S(1)}, u32[]{:S(2)}, u32[]{:S(2)}) collective-permute-start(f32[64,256]{1,0:T(8,128)S(1)} %get-tuple-element.133.refs_4_), channel_id=1, source_target_pairs={{0,1},{1,0},{2,3},{3,2},{4,5},{5,4},{6,7},{7,6},{8,9},{9,8},{10,11... | collective-permute-start | bytes 196616 | tf_op jit(solution)/shard_map/ppermute | solution.py:291
  15.0 0.0 collective-permute-start.2
  15.0 0.7 %inner_blocks.6 = (f32[3,128,256]{2,1,0:T(8,128)S(1)}, f32[4,128,256]{2,1,0:T(8,128)S(1)}, f32[3,128,256]{2,1,0:T(8,128)S(1)}, f32[128,256]{1,0:T(8,128)S(1)}, f32[128,256]{1,0:T(8,128)S(1)}) custom-call(bf16[3,512,256]{2,1,0:T(8,128)(2,1)S(1)} %get-tuple-element.112.own, bf16[3,512,256]{2,1,0:T(8,128)(2,1)S(1)} %get-tuple-element.113.lower, ...), custom_call_target="tpu_custom_call" | custom-call | tf_op jit(solution)/shard_map/inner_blocks/pallas_call | solution.py:322
  15.7 1.8 %collective-permute-done.3.refs_6_ = f32[64,256]{1,0:T(8,128)S(1)} collective-permute-done((f32[64,256]{1,0:T(8,128)S(1)}, f32[64,256]{1,0:T(8,128)S(1)}, u32[]{:S(2)}, u32[]{:S(2)}) %collective-permute-start.3) | collective-permute-done | bytes 65568 | tf_op jit(solution)/shard_map/ppermute | solution.py:291
  17.5 0.0 collective-permute-done.4.refs_7_
  17.5 0.3 edge_blocks.11
  17.9 2.8 %collective-permute-start.7 = (f32[64,256]{1,0:T(8,128)S(1)}, f32[64,256]{1,0:T(8,128)S(1)}, u32[]{:S(2)}, u32[]{:S(2)}) collective-permute-start(f32[64,256]{1,0:T(8,128)S(1)} %get-tuple-element.155.refs_4_), channel_id=1, source_target_pairs={{0,1},{1,0},{2,3},{3,2},{4,5},{5,4},{6,7},{7,6},{8,9},{9,8},{10,11... | collective-permute-start | bytes 196616 | tf_op jit(solution)/shard_map/ppermute | solution.py:291
  20.7 0.0 collective-permute-start.8
  20.7 0.0 collective-permute-done.1.refs_6_
  20.7 0.0 collective-permute-done.2.refs_7_
  20.7 0.3 edge_blocks.10
  21.0 1.3 %collective-permute-start.5 = (f32[64,256]{1,0:T(8,128)S(1)}, f32[64,256]{1,0:T(8,128)S(1)}, u32[]{:S(2)}, u32[]{:S(2)}) collective-permute-start(f32[64,256]{1,0:T(8,128)S(1)} %get-tuple-element.150.refs_4_), channel_id=1, source_target_pairs={{0,1},{1,0},{2,3},{3,2},{4,5},{5,4},{6,7},{7,6},{8,9},{9,8},{10,11... | collective-permute-start | bytes 196616 | tf_op jit(solution)/shard_map/ppermute | solution.py:291
  22.3 0.0 collective-permute-start.6
  22.3 0.7 %inner_blocks.7 = (f32[3,128,256]{2,1,0:T(8,128)S(1)}, f32[4,128,256]{2,1,0:T(8,128)S(1)}, f32[3,128,256]{2,1,0:T(8,128)S(1)}, f32[128,256]{1,0:T(8,128)S(1)}, f32[128,256]{1,0:T(8,128)S(1)}) custom-call(bf16[3,512,256]{2,1,0:T(8,128)(2,1)S(1)} %get-tuple-element.112.own, bf16[3,512,256]{2,1,0:T(8,128)(2,1)S(1)} %get-tuple-element.113.lower, ...), custom_call_target="tpu_custom_call" | custom-call | tf_op jit(solution)/shard_map/inner_blocks/pallas_call | solution.py:322
  23.0 0.0 collective-permute-done.7.refs_6_
  23.0 0.0 collective-permute-done.8.refs_7_
  23.0 0.3 edge_blocks.13
  23.4 3.9 %collective-permute-start.11 = (f32[64,256]{1,0:T(8,128)S(1)}, f32[64,256]{1,0:T(8,128)S(1)}, u32[]{:S(2)}, u32[]{:S(2)}) collective-permute-start(f32[64,256]{1,0:T(8,128)S(1)} %get-tuple-element.172.refs_4_), channel_id=1, source_target_pairs={{0,1},{1,0},{2,3},{3,2},{4,5},{5,4},{6,7},{7,6},{8,9},{9,8},{10,11... | collective-permute-start | bytes 196616 | tf_op jit(solution)/shard_map/ppermute | solution.py:291
  27.3 0.0 collective-permute-start.12
  27.3 0.0 collective-permute-done.5.refs_6_
  27.3 0.0 collective-permute-done.6.refs_7_
  27.3 0.3 edge_blocks.12
  27.6 0.6 %collective-permute-start.10 = (f32[64,256]{1,0:T(8,128)S(1)}, f32[64,256]{1,0:T(8,128)S(1)}, u32[]{:S(2)}, u32[]{:S(2)}) collective-permute-start(f32[64,256]{1,0:T(8,128)S(1)} %get-tuple-element.168.refs_5_), channel_id=1, source_target_pairs={{0,8},{1,2},{2,1},{3,4},{4,3},{5,6},{6,5},{7,15},{8,0},{9,10},{10,... | collective-permute-start | bytes 196616 | tf_op jit(solution)/shard_map/ppermute | solution.py:290
  28.2 4.3 %collective-permute-start.9 = (f32[64,256]{1,0:T(8,128)S(1)}, f32[64,256]{1,0:T(8,128)S(1)}, u32[]{:S(2)}, u32[]{:S(2)}) collective-permute-start(f32[64,256]{1,0:T(8,128)S(1)} %get-tuple-element.167.refs_4_), channel_id=1, source_target_pairs={{0,1},{1,0},{2,3},{3,2},{4,5},{5,4},{6,7},{7,6},{8,9},{9,8},{10,11... | collective-permute-start | bytes 196616 | tf_op jit(solution)/shard_map/ppermute | solution.py:291
  32.4 0.7 %inner_blocks.8 = (f32[3,128,256]{2,1,0:T(8,128)S(1)}, f32[4,128,256]{2,1,0:T(8,128)S(1)}, f32[3,128,256]{2,1,0:T(8,128)S(1)}, f32[128,256]{1,0:T(8,128)S(1)}, f32[128,256]{1,0:T(8,128)S(1)}) custom-call(bf16[3,512,256]{2,1,0:T(8,128)(2,1)S(1)} %get-tuple-element.112.own, bf16[3,512,256]{2,1,0:T(8,128)(2,1)S(1)} %get-tuple-element.113.lower, ...), custom_call_target="tpu_custom_call" | custom-call | tf_op jit(solution)/shard_map/inner_blocks/pallas_call | solution.py:322
  33.2 0.0 collective-permute-done.11.refs_6_
  33.2 0.0 collective-permute-done.12.refs_7_
  33.2 0.3 edge_blocks.15
  33.5 0.2 collective-permute-start.15
  33.7 0.0 collective-permute-start.16
  33.7 0.0 collective-permute-done.10.refs_7_
  33.7 1.0 %collective-permute-done.9.refs_6_ = f32[64,256]{1,0:T(8,128)S(1)} collective-permute-done((f32[64,256]{1,0:T(8,128)S(1)}, f32[64,256]{1,0:T(8,128)S(1)}, u32[]{:S(2)}, u32[]{:S(2)}) %collective-permute-start.9) | collective-permute-done | bytes 65568 | tf_op jit(solution)/shard_map/ppermute | solution.py:291
  34.7 0.3 edge_blocks.14
  35.0 2.1 %collective-permute-start.13 = (f32[64,256]{1,0:T(8,128)S(1)}, f32[64,256]{1,0:T(8,128)S(1)}, u32[]{:S(2)}, u32[]{:S(2)}) collective-permute-start(f32[64,256]{1,0:T(8,128)S(1)} %get-tuple-element.184.refs_4_), channel_id=1, source_target_pairs={{0,1},{1,0},{2,3},{3,2},{4,5},{5,4},{6,7},{7,6},{8,9},{9,8},{10,11... | collective-permute-start | bytes 196616 | tf_op jit(solution)/shard_map/ppermute | solution.py:291
  37.1 0.0 collective-permute-start.14
  37.1 0.7 %inner_blocks.9 = (f32[3,128,256]{2,1,0:T(8,128)S(1)}, f32[4,128,256]{2,1,0:T(8,128)S(1)}, f32[3,128,256]{2,1,0:T(8,128)S(1)}, f32[128,256]{1,0:T(8,128)S(1)}, f32[128,256]{1,0:T(8,128)S(1)}) custom-call(bf16[3,512,256]{2,1,0:T(8,128)(2,1)S(1)} %get-tuple-element.112.own, bf16[3,512,256]{2,1,0:T(8,128)(2,1)S(1)} %get-tuple-element.113.lower, ...), custom_call_target="tpu_custom_call" | custom-call | tf_op jit(solution)/shard_map/inner_blocks/pallas_call | solution.py:322
  37.8 0.6 %collective-permute-done.15.refs_6_ = f32[64,256]{1,0:T(8,128)S(1)} collective-permute-done((f32[64,256]{1,0:T(8,128)S(1)}, f32[64,256]{1,0:T(8,128)S(1)}, u32[]{:S(2)}, u32[]{:S(2)}) %collective-permute-start.15) | collective-permute-done | bytes 65568 | tf_op jit(solution)/shard_map/ppermute | solution.py:291
  38.5 0.0 collective-permute-done.16.refs_7_
  38.5 0.3 edge_blocks.17
  38.8 2.9 %collective-permute-start.19 = (f32[64,256]{1,0:T(8,128)S(1)}, f32[64,256]{1,0:T(8,128)S(1)}, u32[]{:S(2)}, u32[]{:S(2)}) collective-permute-start(f32[64,256]{1,0:T(8,128)S(1)} %get-tuple-element.206.refs_4_), channel_id=1, source_target_pairs={{0,1},{1,0},{2,3},{3,2},{4,5},{5,4},{6,7},{7,6},{8,9},{9,8},{10,11... | collective-permute-start | bytes 196616 | tf_op jit(solution)/shard_map/ppermute | solution.py:291
  41.7 0.0 collective-permute-start.20
  41.7 0.0 collective-permute-done.13.refs_6_
  41.7 0.0 collective-permute-done.14.refs_7_
  41.7 0.3 edge_blocks.16
  42.0 1.4 %collective-permute-start.17 = (f32[64,256]{1,0:T(8,128)S(1)}, f32[64,256]{1,0:T(8,128)S(1)}, u32[]{:S(2)}, u32[]{:S(2)}) collective-permute-start(f32[64,256]{1,0:T(8,128)S(1)} %get-tuple-element.201.refs_4_), channel_id=1, source_target_pairs={{0,1},{1,0},{2,3},{3,2},{4,5},{5,4},{6,7},{7,6},{8,9},{9,8},{10,11... | collective-permute-start | bytes 196616 | tf_op jit(solution)/shard_map/ppermute | solution.py:291
  43.4 0.0 collective-permute-start.18
  43.4 0.7 %inner_blocks.10 = (f32[3,128,256]{2,1,0:T(8,128)S(1)}, f32[4,128,256]{2,1,0:T(8,128)S(1)}, f32[3,128,256]{2,1,0:T(8,128)S(1)}, f32[128,256]{1,0:T(8,128)S(1)}, f32[128,256]{1,0:T(8,128)S(1)}) custom-call(bf16[3,512,256]{2,1,0:T(8,128)(2,1)S(1)} %get-tuple-element.112.own, bf16[3,512,256]{2,1,0:T(8,128)(2,1)S(1)} %get-tuple-element.113.lower, ...), custom_call_target="tpu_custom_call" | custom-call | tf_op jit(solution)/shard_map/inner_blocks/pallas_call | solution.py:322
  44.1 0.0 collective-permute-done.19.refs_6_
  44.1 0.0 collective-permute-done.20.refs_7_
  44.1 0.3 edge_blocks.19
  44.5 2.9 %collective-permute-start.22 = (f32[64,256]{1,0:T(8,128)S(1)}, f32[64,256]{1,0:T(8,128)S(1)}, u32[]{:S(2)}, u32[]{:S(2)}) collective-permute-start(f32[64,256]{1,0:T(8,128)S(1)} %get-tuple-element.219), channel_id=1, source_target_pairs={{1,0},{2,1},{3,2},{4,3},{5,4},{6,5},{7,6},{0,7},{9,8},{10,9},{11,1... | collective-permute-start | bytes 196616 | tf_op jit(solution)/shard_map/ppermute | solution.py:316
  47.4 0.0 collective-permute-done.17.refs_6_
  47.4 0.3 edge_blocks.18
  47.7 2.4 %collective-permute-start.21 = (f32[64,256]{1,0:T(8,128)S(1)}, f32[64,256]{1,0:T(8,128)S(1)}, u32[]{:S(2)}, u32[]{:S(2)}) collective-permute-start(f32[64,256]{1,0:T(8,128)S(1)} %get-tuple-element.218), channel_id=1, source_target_pairs={{1,0},{2,1},{3,2},{4,3},{5,4},{6,5},{7,6},{0,7},{9,8},{10,9},{11,1... | collective-permute-start | bytes 196616 | tf_op jit(solution)/shard_map/ppermute | solution.py:316
  50.1 1.4 %inner_blocks.11 = (f32[3,256,128]{2,1,0:T(8,128)S(1)}, f32[4,256,128]{2,1,0:T(8,128)}) custom-call(bf16[3,512,256]{2,1,0:T(8,128)(2,1)S(1)} %get-tuple-element.112.own, bf16[3,512,256]{2,1,0:T(8,128)(2,1)S(1)} %get-tuple-element.113.lower, bf16[3,512,256]{2,1,0:T(8,128)(2,1)S(1)} %get-tuple-element.114.upper, f32[8,8,256]{2,1,0:T(8,128)S(1)} %get-tuple-element.115.marks, ...), custom_call_target="tpu_custom_call" | custom-call | tf_op jit(solution)/shard_map/inner_blocks/pallas_call | solution.py:322
  51.5 1.1 %collective-permute-done.21.refs_4_ = f32[64,256]{1,0:T(8,128)S(1)} collective-permute-done((f32[64,256]{1,0:T(8,128)S(1)}, f32[64,256]{1,0:T(8,128)S(1)}, u32[]{:S(2)}, u32[]{:S(2)}) %collective-permute-start.21) | collective-permute-done | bytes 65568 | tf_op jit(solution)/shard_map/ppermute | solution.py:316
  52.6 0.9 %last_residual.1 = f32[1,1,4,256,128]{4,3,2,1,0:T(8,128)} custom-call(f32[8,8,256]{2,1,0:T(8,128)S(1)} %get-tuple-element.115.marks, f32[3,256,128]{2,1,0:T(8,128)S(1)} %get-tuple-element.213.residual, f32[64,256]{1,0:T(8,128)S(1)} %get-tuple-element.214.refs_0_, f32[64,256]{1,0:T(8,128)S(1)} %get-tuple-element.215.refs_1_, ...), custom_call_target="tpu_custom_call" | custom-call | tf_op jit(solution)/shard_map/last_residual/pallas_call | solution.py:337
  (5 shorter events, 0.0 us)
Async XLA Ops:
  0.6 5.3 %copy-start = (f32[1,1,4,512,512]{4,3,2,1,0:T(8,128)S(1)}, f32[1,1,4,512,512]{4,3,2,1,0:T(8,128)}, u32[]{:S(2)}) copy-start(f32[1,1,4,512,512]{4,3,2,1,0:T(8,128)} %operators.3) | copy-start | bytes 12582916
  2.9 9.6 %collective-permute-start = (f32[128,256]{1,0:T(8,128)S(1)}, f32[128,256]{1,0:T(8,128)S(1)}, u32[]{:S(2)}, u32[]{:S(2)}) collective-permute-start(f32[128,256]{1,0:T(8,128)S(1)} %get-tuple-element.120.ends), channel_id=1, source_target_pairs={{0,1},{1,2},{2,3},{3,4},{4,5},{5,6},{6,7},{7,0},{8,9},{9,10},{10,1... | collective-permute-start | bytes 393224 | tf_op jit(solution)/shard_map/ppermute | solution.py:302
  12.9 4.7 %collective-permute-start.3 = (f32[64,256]{1,0:T(8,128)S(1)}, f32[64,256]{1,0:T(8,128)S(1)}, u32[]{:S(2)}, u32[]{:S(2)}) collective-permute-start(f32[64,256]{1,0:T(8,128)S(1)} %get-tuple-element.138.refs_4_), channel_id=1, source_target_pairs={{0,1},{1,0},{2,3},{3,2},{4,5},{5,4},{6,7},{7,6},{8,9},{9,8},{10,11... | collective-permute-start | bytes 196616 | tf_op jit(solution)/shard_map/ppermute | solution.py:291
  12.9 4.6 %collective-permute-start.4 = (f32[64,256]{1,0:T(8,128)S(1)}, f32[64,256]{1,0:T(8,128)S(1)}, u32[]{:S(2)}, u32[]{:S(2)}) collective-permute-start(f32[64,256]{1,0:T(8,128)S(1)} %get-tuple-element.139.refs_5_), channel_id=1, source_target_pairs={{0,8},{1,2},{2,1},{3,4},{4,3},{5,6},{6,5},{7,15},{8,0},{9,10},{10,... | collective-permute-start | bytes 196616 | tf_op jit(solution)/shard_map/ppermute | solution.py:290
  13.0 7.6 %collective-permute-start.1 = (f32[64,256]{1,0:T(8,128)S(1)}, f32[64,256]{1,0:T(8,128)S(1)}, u32[]{:S(2)}, u32[]{:S(2)}) collective-permute-start(f32[64,256]{1,0:T(8,128)S(1)} %get-tuple-element.133.refs_4_), channel_id=1, source_target_pairs={{0,1},{1,0},{2,3},{3,2},{4,5},{5,4},{6,7},{7,6},{8,9},{9,8},{10,11... | collective-permute-start | bytes 196616 | tf_op jit(solution)/shard_map/ppermute | solution.py:291
  15.0 5.7 %collective-permute-start.2 = (f32[64,256]{1,0:T(8,128)S(1)}, f32[64,256]{1,0:T(8,128)S(1)}, u32[]{:S(2)}, u32[]{:S(2)}) collective-permute-start(f32[64,256]{1,0:T(8,128)S(1)} %get-tuple-element.134.refs_5_), channel_id=1, source_target_pairs={{0,8},{1,2},{2,1},{3,4},{4,3},{5,6},{6,5},{7,15},{8,0},{9,10},{10,... | collective-permute-start | bytes 196616 | tf_op jit(solution)/shard_map/ppermute | solution.py:290
  17.9 5.2 %collective-permute-start.7 = (f32[64,256]{1,0:T(8,128)S(1)}, f32[64,256]{1,0:T(8,128)S(1)}, u32[]{:S(2)}, u32[]{:S(2)}) collective-permute-start(f32[64,256]{1,0:T(8,128)S(1)} %get-tuple-element.155.refs_4_), channel_id=1, source_target_pairs={{0,1},{1,0},{2,3},{3,2},{4,5},{5,4},{6,7},{7,6},{8,9},{9,8},{10,11... | collective-permute-start | bytes 196616 | tf_op jit(solution)/shard_map/ppermute | solution.py:291
  20.7 2.4 %collective-permute-start.8 = (f32[64,256]{1,0:T(8,128)S(1)}, f32[64,256]{1,0:T(8,128)S(1)}, u32[]{:S(2)}, u32[]{:S(2)}) collective-permute-start(f32[64,256]{1,0:T(8,128)S(1)} %get-tuple-element.156.refs_5_), channel_id=1, source_target_pairs={{0,8},{1,2},{2,1},{3,4},{4,3},{5,6},{6,5},{7,15},{8,0},{9,10},{10,... | collective-permute-start | bytes 196616 | tf_op jit(solution)/shard_map/ppermute | solution.py:290
  21.0 6.3 %collective-permute-start.5 = (f32[64,256]{1,0:T(8,128)S(1)}, f32[64,256]{1,0:T(8,128)S(1)}, u32[]{:S(2)}, u32[]{:S(2)}) collective-permute-start(f32[64,256]{1,0:T(8,128)S(1)} %get-tuple-element.150.refs_4_), channel_id=1, source_target_pairs={{0,1},{1,0},{2,3},{3,2},{4,5},{5,4},{6,7},{7,6},{8,9},{9,8},{10,11... | collective-permute-start | bytes 196616 | tf_op jit(solution)/shard_map/ppermute | solution.py:291
  22.3 5.0 %collective-permute-start.6 = (f32[64,256]{1,0:T(8,128)S(1)}, f32[64,256]{1,0:T(8,128)S(1)}, u32[]{:S(2)}, u32[]{:S(2)}) collective-permute-start(f32[64,256]{1,0:T(8,128)S(1)} %get-tuple-element.151.refs_5_), channel_id=1, source_target_pairs={{0,8},{1,2},{2,1},{3,4},{4,3},{5,6},{6,5},{7,15},{8,0},{9,10},{10,... | collective-permute-start | bytes 196616 | tf_op jit(solution)/shard_map/ppermute | solution.py:290
  23.4 9.8 %collective-permute-start.11 = (f32[64,256]{1,0:T(8,128)S(1)}, f32[64,256]{1,0:T(8,128)S(1)}, u32[]{:S(2)}, u32[]{:S(2)}) collective-permute-start(f32[64,256]{1,0:T(8,128)S(1)} %get-tuple-element.172.refs_4_), channel_id=1, source_target_pairs={{0,1},{1,0},{2,3},{3,2},{4,5},{5,4},{6,7},{7,6},{8,9},{9,8},{10,11... | collective-permute-start | bytes 196616 | tf_op jit(solution)/shard_map/ppermute | solution.py:291
  27.3 5.9 %collective-permute-start.12 = (f32[64,256]{1,0:T(8,128)S(1)}, f32[64,256]{1,0:T(8,128)S(1)}, u32[]{:S(2)}, u32[]{:S(2)}) collective-permute-start(f32[64,256]{1,0:T(8,128)S(1)} %get-tuple-element.173.refs_5_), channel_id=1, source_target_pairs={{0,8},{1,2},{2,1},{3,4},{4,3},{5,6},{6,5},{7,15},{8,0},{9,10},{10,... | collective-permute-start | bytes 196616 | tf_op jit(solution)/shard_map/ppermute | solution.py:290
  27.6 6.1 %collective-permute-start.10 = (f32[64,256]{1,0:T(8,128)S(1)}, f32[64,256]{1,0:T(8,128)S(1)}, u32[]{:S(2)}, u32[]{:S(2)}) collective-permute-start(f32[64,256]{1,0:T(8,128)S(1)} %get-tuple-element.168.refs_5_), channel_id=1, source_target_pairs={{0,8},{1,2},{2,1},{3,4},{4,3},{5,6},{6,5},{7,15},{8,0},{9,10},{10,... | collective-permute-start | bytes 196616 | tf_op jit(solution)/shard_map/ppermute | solution.py:290
  28.2 6.5 %collective-permute-start.9 = (f32[64,256]{1,0:T(8,128)S(1)}, f32[64,256]{1,0:T(8,128)S(1)}, u32[]{:S(2)}, u32[]{:S(2)}) collective-permute-start(f32[64,256]{1,0:T(8,128)S(1)} %get-tuple-element.167.refs_4_), channel_id=1, source_target_pairs={{0,1},{1,0},{2,3},{3,2},{4,5},{5,4},{6,7},{7,6},{8,9},{9,8},{10,11... | collective-permute-start | bytes 196616 | tf_op jit(solution)/shard_map/ppermute | solution.py:291
  33.5 5.0 %collective-permute-start.15 = (f32[64,256]{1,0:T(8,128)S(1)}, f32[64,256]{1,0:T(8,128)S(1)}, u32[]{:S(2)}, u32[]{:S(2)}) collective-permute-start(f32[64,256]{1,0:T(8,128)S(1)} %get-tuple-element.189.refs_4_), channel_id=1, source_target_pairs={{0,1},{1,0},{2,3},{3,2},{4,5},{5,4},{6,7},{7,6},{8,9},{9,8},{10,11... | collective-permute-start | bytes 196616 | tf_op jit(solution)/shard_map/ppermute | solution.py:291
  33.7 4.8 %collective-permute-start.16 = (f32[64,256]{1,0:T(8,128)S(1)}, f32[64,256]{1,0:T(8,128)S(1)}, u32[]{:S(2)}, u32[]{:S(2)}) collective-permute-start(f32[64,256]{1,0:T(8,128)S(1)} %get-tuple-element.190.refs_5_), channel_id=1, source_target_pairs={{0,8},{1,2},{2,1},{3,4},{4,3},{5,6},{6,5},{7,15},{8,0},{9,10},{10,... | collective-permute-start | bytes 196616 | tf_op jit(solution)/shard_map/ppermute | solution.py:290
  35.0 6.7 %collective-permute-start.13 = (f32[64,256]{1,0:T(8,128)S(1)}, f32[64,256]{1,0:T(8,128)S(1)}, u32[]{:S(2)}, u32[]{:S(2)}) collective-permute-start(f32[64,256]{1,0:T(8,128)S(1)} %get-tuple-element.184.refs_4_), channel_id=1, source_target_pairs={{0,1},{1,0},{2,3},{3,2},{4,5},{5,4},{6,7},{7,6},{8,9},{9,8},{10,11... | collective-permute-start | bytes 196616 | tf_op jit(solution)/shard_map/ppermute | solution.py:291
  37.1 4.6 %collective-permute-start.14 = (f32[64,256]{1,0:T(8,128)S(1)}, f32[64,256]{1,0:T(8,128)S(1)}, u32[]{:S(2)}, u32[]{:S(2)}) collective-permute-start(f32[64,256]{1,0:T(8,128)S(1)} %get-tuple-element.185.refs_5_), channel_id=1, source_target_pairs={{0,8},{1,2},{2,1},{3,4},{4,3},{5,6},{6,5},{7,15},{8,0},{9,10},{10,... | collective-permute-start | bytes 196616 | tf_op jit(solution)/shard_map/ppermute | solution.py:290
  38.8 5.3 %collective-permute-start.19 = (f32[64,256]{1,0:T(8,128)S(1)}, f32[64,256]{1,0:T(8,128)S(1)}, u32[]{:S(2)}, u32[]{:S(2)}) collective-permute-start(f32[64,256]{1,0:T(8,128)S(1)} %get-tuple-element.206.refs_4_), channel_id=1, source_target_pairs={{0,1},{1,0},{2,3},{3,2},{4,5},{5,4},{6,7},{7,6},{8,9},{9,8},{10,11... | collective-permute-start | bytes 196616 | tf_op jit(solution)/shard_map/ppermute | solution.py:291
  41.7 2.4 %collective-permute-start.20 = (f32[64,256]{1,0:T(8,128)S(1)}, f32[64,256]{1,0:T(8,128)S(1)}, u32[]{:S(2)}, u32[]{:S(2)}) collective-permute-start(f32[64,256]{1,0:T(8,128)S(1)} %get-tuple-element.207.refs_5_), channel_id=1, source_target_pairs={{0,8},{1,2},{2,1},{3,4},{4,3},{5,6},{6,5},{7,15},{8,0},{9,10},{10,... | collective-permute-start | bytes 196616 | tf_op jit(solution)/shard_map/ppermute | solution.py:290
  42.0 5.3 %collective-permute-start.17 = (f32[64,256]{1,0:T(8,128)S(1)}, f32[64,256]{1,0:T(8,128)S(1)}, u32[]{:S(2)}, u32[]{:S(2)}) collective-permute-start(f32[64,256]{1,0:T(8,128)S(1)} %get-tuple-element.201.refs_4_), channel_id=1, source_target_pairs={{0,1},{1,0},{2,3},{3,2},{4,5},{5,4},{6,7},{7,6},{8,9},{9,8},{10,11... | collective-permute-start | bytes 196616 | tf_op jit(solution)/shard_map/ppermute | solution.py:291
  43.4 4.0 %collective-permute-start.18 = (f32[64,256]{1,0:T(8,128)S(1)}, f32[64,256]{1,0:T(8,128)S(1)}, u32[]{:S(2)}, u32[]{:S(2)}) collective-permute-start(f32[64,256]{1,0:T(8,128)S(1)} %get-tuple-element.202.refs_5_), channel_id=1, source_target_pairs={{0,8},{1,2},{2,1},{3,4},{4,3},{5,6},{6,5},{7,15},{8,0},{9,10},{10,... | collective-permute-start | bytes 196616 | tf_op jit(solution)/shard_map/ppermute | solution.py:290
  44.5 7.0 %collective-permute-start.22 = (f32[64,256]{1,0:T(8,128)S(1)}, f32[64,256]{1,0:T(8,128)S(1)}, u32[]{:S(2)}, u32[]{:S(2)}) collective-permute-start(f32[64,256]{1,0:T(8,128)S(1)} %get-tuple-element.219), channel_id=1, source_target_pairs={{1,0},{2,1},{3,2},{4,3},{5,4},{6,5},{7,6},{0,7},{9,8},{10,9},{11,1... | collective-permute-start | bytes 196616 | tf_op jit(solution)/shard_map/ppermute | solution.py:316
  47.7 4.9 %collective-permute-start.21 = (f32[64,256]{1,0:T(8,128)S(1)}, f32[64,256]{1,0:T(8,128)S(1)}, u32[]{:S(2)}, u32[]{:S(2)}) collective-permute-start(f32[64,256]{1,0:T(8,128)S(1)} %get-tuple-element.218), channel_id=1, source_target_pairs={{1,0},{2,1},{3,2},{4,3},{5,4},{6,5},{7,6},{0,7},{9,8},{10,9},{11,1... | collective-permute-start | bytes 196616 | tf_op jit(solution)/shard_map/ppermute | solution.py:316
where the time goes:
time: 53.7 us; the launch traced here: 53.5 us
  starting transfers between devices  29.9 us (56%)
  Pallas kernels  14.5 us (27%)
  waiting for transfers between devices  7.46 us (14%)
  between operations  1.67 us (3%)
    ppermute x10, starting transfers between devices, exchange(): even = lax.ppermute(even, ('grp', 'sub'), evens)  20.9 us
    ppermute x2, starting transfers between devices, shards(): came = [lax.ppermute(state[4], 'sub', backward) for state in states]  5.3 us
    pallas_call x6, Pallas kernels, shards(): call(functools.partial(inner_kernel, factors, PARTS), 'inner_blocks', [VM...  4.86 us
    pallas_call x1, Pallas kernels, shards(): call(operator_kernel, 'block_operators', [SMEM, VMEM, VMEM], [matrices] *...  3.67 us
    ppermute x10, waiting for transfers between devices, exchange(): even = lax.ppermute(even, ('grp', 'sub'), evens)  3.45 us
    pallas_call x10, Pallas kernels, shards(): call(functools.partial(edge_kernel, factors, slots, k * width, step == IT...  3.18 us
    ppermute x1, starting transfers between devices, shards(): before = lax.ppermute(ends, 'sub', forward)  3.02 us
    ppermute x1, waiting for transfers between devices, shards(): before = lax.ppermute(ends, 'sub', forward)  2.86 us
  transfers between devices with their start and end apart: 23, of which 5 were waited for; matrix products, arithmetic and copies ran while one was open for 0% of the time, Pallas kernels for 22%

commit v1 on v0

--- a/solution.py
+++ b/solution.py
@@ -16,7 +16,7 @@
 F32 = jnp.float32
 PARTS = 2
 VMEM_BYTES = 24 * 1024 * 1024
-FIRST_VMEM_BYTES = 51 * 1024 * 1024
+FIRST_VMEM_BYTES = 52 * 1024 * 1024
 
 
 def chebyshev_factors():
@@ -65,16 +65,18 @@
     return tall[:rows] + tall[rows:] + jnp.dot(high, matrix[h:], preferred_element_type=F32)
 
 
+def beside(x, y):
+    return tuple(jnp.concatenate(pair, axis=1) for pair in zip(x, y))
+
+
 def dot_nt(a, b):
     return lax.dot_general(a, b, (((1,), (1,)), ((), ())), preferred_element_type=F32)
 
 
-def signed_placement(pairs):
+def signed_placement(pairs, scale):
     h = pairs.shape[1]
     rows = lax.broadcasted_iota(jnp.int32, (h, h), 0)
-    picked = jnp.abs(pairs) - 1
-    sign = jnp.where(pairs > 0, 1.0, -1.0)
-    return jnp.where(rows == picked, sign, 0.0).astype(BF16)
+    return jnp.where(rows == jnp.abs(pairs) - 1, jnp.where(pairs > 0, scale, -scale), 0.0).astype(BF16)
 
 
 def row(marks, k):
@@ -85,16 +87,16 @@
     return dict(even=slots, alone=slots + 1, evens=slots + 2, odds=slots + 3)
 
 
-def first_kernel(owners, counts, operators, pairs, gap, residual, direction, ends, beside_even, beside_odd, marks, pairs_out, source, sems):
-    slots = source.shape[0]
+def first_kernel(owners, counts, operators, pairs, gap, ends, marks, pairs_out, source, sems):
+    slots = pairs_out.shape[0]
+    count = counts[0, 0]
     copies = [
-        pltpu.make_async_copy(gap.at[0, 0], source, sems.at[0]),
+        pltpu.make_async_copy(gap.at[0, 0, count - 1], source, sems.at[0]),
         pltpu.make_async_copy(pairs.at[0, 0], pairs_out, sems.at[1]),
     ]
     for copy in copies:
         copy.start()
     pos = lax.axis_index("sub")
-    count = counts[0, 0]
     is_even = lax.rem(pos, 2) == 0
     place = mark_places(slots)
     has_left, has_right = pos > 0, pos < owners - 1
@@ -106,11 +108,7 @@
     for k, flag in enumerate(flags):
         marks[k] = jnp.full(marks.shape[1:], jnp.where(flag, 1.0, 0.0), F32)
     copies[0].wait()
-    ends[...] = source[count - 1].T * jnp.where(has_right, 1.0, 0.0)
-    for j in range(slots - 1):
-        residual[j] = source[j].T * jnp.where(j < count - 1, 1.0, 0.0)
-        direction[j] = residual[j] / CENTRE
-    put_beside(marks, slots, [direction[j] for j in range(slots - 1)], beside_even, beside_odd)
+    ends[...] = source[...].T * jnp.where(has_right, 1.0, 0.0)
     copies[1].wait()
 
 
@@ -121,50 +119,66 @@
     beside_odd[...] = jnp.where(is_even, first, before_last)
 
 
-def operator_kernel(counts, operators, pairs, own_out, lower_out, upper_out, even_out, odd_out):
+def operator_kernel(counts, operators, pairs, marks, gap, own_out, lower_out, upper_out, even_out, odd_out, residual, direction, beside_even, beside_odd, source, sem):
     slots, h = pairs.shape
     count = counts[0, 0]
+    copy = pltpu.make_async_copy(gap.at[0, 0, pl.ds(0, slots - 1)], source, sem)
+    copy.start()
     is_even = lax.rem(lax.axis_index("sub"), 2) == 0
-    unit = signed_placement(lax.broadcasted_iota(jnp.int32, (1, h), 1) + 1)
+    low = pl.ds(h, h)
     for j in range(slots):
-        place = signed_placement(pairs[pl.ds(j, 1), :])
-        between = jnp.where(j < count - 1, 1.0, 0.0)
-        squares, diagonal, lowers, uppers = [], [], [], []
-        for part in halves(operators[0, 0, j]):
-            placed = jnp.dot(place, part[:h], preferred_element_type=F32).astype(BF16)
-            uppers.append(-dot_nt(unit, placed[:, h:]).astype(BF16))
-            lowers.append(-dot_nt(place, part[h:, :h]))
-            squares.append(dot_nt(place, placed[:, :h]))
-            diagonal.append(dot_nt(unit, part[h:, h:]))
-        for k in range(2):
-            rows = pl.ds(k * h, h)
-            if j < slots - 1:
-                lower_out[j, rows, :] = (lowers[k] * between).astype(BF16)
-            if j > 0:
-                upper_out[j - 1, rows, :] = uppers[k]
-
-            def put_end(out, square, other, rows=rows, k=k):
-                out[0, rows, :] = square[k].astype(BF16)
-                out[1, rows, :] = other[k].astype(BF16)
-
-            if j == 0:
-                pl.when(is_even)(functools.partial(put_end, odd_out, squares, uppers))
-                pl.when(~is_even)(functools.partial(put_end, even_out, squares, uppers))
-            is_last = count - 1 == j
-            pl.when(jnp.logical_and(is_last, is_even))(functools.partial(put_end, even_out, diagonal, lowers))
-            pl.when(jnp.logical_and(is_last, ~is_even))(functools.partial(put_end, odd_out, diagonal, lowers))
+        row_pairs = pairs[pl.ds(j, 1), :]
+        place = signed_placement(row_pairs, 1.0)
+        parts = halves(operators[0, 0, j])
+        placed = [jnp.dot(place, part[:h], preferred_element_type=F32) for part in parts]
+        uppers = [(-part[:, h:]).T.astype(BF16) for part in placed]
+        placed = [part[:, :h].astype(BF16) for part in placed]
         if j > 0:
-            summed = (previous + (squares[0] + squares[1])) * jnp.where(j < count, 1.0, 0.0)
-            own_out[j - 1, pl.ds(0, h), :], own_out[j - 1, pl.ds(h, h), :] = halves(summed)
-        previous = diagonal[0] + diagonal[1]
+            live = jnp.where(j < count, 1.0, 0.0)
+            scaled = signed_placement(row_pairs, live)
+            square = dot_nt(jnp.concatenate([scaled, scaled], axis=1), jnp.concatenate(placed, axis=1))
+            put_halves(own_out, j - 1, square + operators[0, 0, j - 1, low, low].T * live)
+            upper_out[j - 1, pl.ds(0, h), :], upper_out[j - 1, low, :] = uppers
+        if j < slots - 1:
+            scaled = signed_placement(row_pairs, jnp.where(j < count - 1, -1.0, 0.0))
+            for k, part in enumerate(parts):
+                lower_out[j, pl.ds(k * h, h), :] = dot_nt(scaled, part[h:, :h]).astype(BF16)
+
+        def put_first(out, place=place, placed=placed, uppers=uppers):
+            for k in range(2):
+                out[pl.ds(2 * k * h, h), :] = dot_nt(place, placed[k]).astype(BF16)
+                out[pl.ds((2 * k + 1) * h, h), :] = uppers[k]
+
+        def put_last(out, j=j, row_pairs=row_pairs, parts=parts):
+            out[pl.ds(0, h), :], out[pl.ds(2 * h, h), :] = halves(operators[0, 0, j, low, low].T)
+            turned = signed_placement(row_pairs, -1.0)
+            for k, part in enumerate(parts):
+                out[pl.ds((2 * k + 1) * h, h), :] = dot_nt(turned, part[h:, :h]).astype(BF16)
+
+        if j == 0:
+            pl.when(is_even)(functools.partial(put_first, odd_out))
+            pl.when(~is_even)(functools.partial(put_first, even_out))
+        is_last = count - 1 == j
+        pl.when(jnp.logical_and(is_last, is_even))(functools.partial(put_last, even_out))
+        pl.when(jnp.logical_and(is_last, ~is_even))(functools.partial(put_last, odd_out))
+    copy.wait()
+    for j in range(slots - 1):
+        residual[j] = source[j].T * jnp.where(j < count - 1, 1.0, 0.0)
+        direction[j] = residual[j] / CENTRE
+    put_beside(marks, slots, [direction[j] for j in range(slots - 1)], beside_even, beside_odd)
+
+
+def put_halves(out, j, matrix):
+    h = matrix.shape[0]
+    out[j, pl.ds(0, h), :], out[j, pl.ds(h, h), :] = halves(matrix)
 
 
 def give(marks, slots, even, odd, beside_even, beside_odd, even_operator, odd_operator):
     alone = row(marks, mark_places(slots)["alone"]) > 0.5
     next_even, next_odd = jnp.where(alone, odd, beside_even), jnp.where(alone, even, beside_odd)
     return (
-        split_dot(operand(even), even_operator[0]) + split_dot(operand(next_even), even_operator[1]),
-        split_dot(operand(odd), odd_operator[0]) + split_dot(operand(next_odd), odd_operator[1]),
+        split_dot(beside(operand(even), operand(next_even)), even_operator[...]),
+        split_dot(beside(operand(odd), operand(next_odd)), odd_operator[...]),
     )
 
 
@@ -202,7 +216,6 @@
 
 
 def inner_kernel(factors, parts, own, lower, upper, marks, direction, residual, *rest):
-    rest = list(rest)
     inner = residual.shape[0]
     slots = inner + 1
     even = jnp.concatenate([ref[...] for ref in rest[:parts]], axis=0)
@@ -212,44 +225,52 @@
     last, before = jnp.where(is_even, even, odd), jnp.where(is_even, odd, even)
     blocks = [row(marks, j) * last + (direction[j] if j < inner else 0.0) for j in range(slots)]
     cases = [operand(block) for block in blocks]
-    residual_out, total_out = outs[:2]
+    if factors is None:
+        residual_out, total_out, residual_ready, total_ready, sems = outs
+        pairs = ((total_ready, total_out), (residual_ready, residual_out))
+        copies = [[pltpu.make_async_copy(x.at[j], y.at[0, 0, j], sems.at[n, j]) for j in range(slots)] for n, (x, y) in enumerate(pairs)]
+    else:
+        residual_out, total_out = outs[:2]
     for j in range(slots):
         summed = total[j] + blocks[j]
-        total_out[j] = summed if factors is not None else summed.T
+        if factors is None:
+            total_ready[j] = summed.T
+            copies[0][j].start()
+        else:
+            total_out[j] = summed
     nexts = []
     for j in range(inner):
         image = split_dot(cases[j], own[j]) + split_dot(cases[j + 1], upper[j])
         image += split_dot(cases[j - 1] if j > 0 else operand(before), lower[j])
         left_over = residual[j] - image
         if factors is None:
-            residual_out[j] = left_over.T
+            residual_ready[j] = left_over.T
+            copies[1][j].start()
             continue
         residual_out[j] = left_over
         nexts.append(factors[0] * direction[j] + factors[1] * left_over)
         outs[2][j] = nexts[j]
     if factors is not None:
         put_beside(marks, slots, nexts, outs[3], outs[4])
-
-
-def last_kernel(parts, marks, residual, *refs):
-    out, ready, sems = refs[3 * parts :]
-    inner = residual.shape[0]
-    slots = inner + 1
+    else:
+        residual_ready[inner] = jnp.zeros(residual_ready.shape[1:], F32)
+        copies[1][inner].start()
+        for copy in copies[0] + copies[1]:
+            copy.wait()
+
+
+def last_kernel(parts, slots, counts, marks, _, *refs):
+    out, ready, sem = refs[3 * parts :]
     place = mark_places(slots)
     last_r, last_given, came = (
         jnp.concatenate([ref[...] for ref in refs[n * parts : (n + 1) * parts]], axis=0) for n in range(3)
     )
     is_even = row(marks, place["even"]) > 0.5
     shared = jnp.where(is_even, row(marks, place["evens"]), row(marks, place["odds"]))
-    last = ((last_r - (last_given + came)) * shared).T
-    copies = []
-    for j in range(slots):
-        mine = marks[j, pl.ds(0, 1), pl.ds(0, last.shape[1])] * last
-        ready[j] = mine + residual[j] if j < inner else mine
-        copies.append(pltpu.make_async_copy(ready.at[j], out.at[0, 0, j], sems.at[j]))
-        copies[j].start()
-    for copy in copies:
-        copy.wait()
+    ready[...] = ((last_r - (last_given + came)) * shared).T
+    copy = pltpu.make_async_copy(ready, out.at[0, 0, counts[0, 0] - 1], sem)
+    copy.start()
+    copy.wait()
 
 
 VMEM = pl.BlockSpec(memory_space=pltpu.VMEM)
@@ -261,13 +282,14 @@
     return pltpu.with_memory_space_constraint(x, pltpu.HBM)
 
 
-def call(kernel, name, ins, outs, scratch=(), out_space=VMEM, vmem=VMEM_BYTES):
+def call(kernel, name, ins, outs, scratch=(), out_space=VMEM, vmem=VMEM_BYTES, aliases=None):
     return pl.pallas_call(
         kernel,
         in_specs=ins,
         out_specs=[out_space] * len(outs),
         out_shape=[jax.ShapeDtypeStruct(shape, kind) for shape, kind in outs],
         scratch_shapes=list(scratch),
+        input_output_aliases=aliases or {},
         compiler_params=pltpu.CompilerParams(vmem_limit_bytes=vmem),
         name=name,
     )
@@ -284,28 +306,30 @@
     block = ((cases, h), F32)
     part = ((width, h), F32)
     matrices = ((slots - 1, 2 * h, h), BF16)
-    pair = ((2, 2 * h, h), BF16)
+    pair = ((4 * h, h), BF16)
 
     def exchange(even, odd):
         odd = lax.ppermute(odd, ("grp", "sub"), odds)
         even = lax.ppermute(even, ("grp", "sub"), evens)
         return even, odd
 
-    residual, direction, ends, *beside, marks, pairs = call(
+    gap = in_hbm(gap)
+    ends, marks, pairs = call(
         functools.partial(first_kernel, owners),
-        "first_blocks",
+        "first_ends",
         [SMEM, HBM, HBM, HBM],
-        [inner, inner, block, block, block, ((slots + 4, 8, h), F32), ((slots, h), jnp.int32)],
-        [pltpu.VMEM((slots, h, cases), F32), pltpu.SemaphoreType.DMA((2,))],
+        [block, ((slots + 4, 8, h), F32), ((slots, h), jnp.int32)],
+        [pltpu.VMEM((h, cases), F32), pltpu.SemaphoreType.DMA((2,))],
         vmem=FIRST_VMEM_BYTES,
-    )(counts, operators, in_hbm(pair_rows), in_hbm(gap))
+    )(counts, operators, in_hbm(pair_rows), gap)
     before = lax.ppermute(ends, "sub", forward)
-    own, lower, upper, even_operator, odd_operator = call(
+    own, lower, upper, even_operator, odd_operator, residual, direction, *beside = call(
         operator_kernel,
         "block_operators",
-        [SMEM, VMEM, VMEM],
-        [matrices] * 3 + [pair] * 2,
-    )(counts, operators, pairs)
+        [SMEM, VMEM, VMEM, VMEM, HBM],
+        [matrices] * 3 + [pair] * 2 + [inner] * 2 + [block] * 2,
+        [pltpu.VMEM((slots - 1, h, cases), F32), pltpu.SemaphoreType.DMA],
+    )(counts, operators, pairs, marks, gap)
     got = call(
         functools.partial(first_edge_kernel, slots, PARTS), "first_edges", [VMEM] * 7, [part] * (6 * PARTS)
     )(even_operator, odd_operator, marks, ends, before, *beside)
@@ -318,9 +342,15 @@
             came = [exchange(state[4], state[5]) for state in states]
         outs = [inner, field, inner, block, block]
         if factors is None:
-            outs = [((slots - 1, h, cases), F32), ((slots, h, cases), F32)]
+            outs = [(gap.shape, F32)] * 2
+        turned = pltpu.VMEM((slots, h, cases), F32)
         got = call(
-            functools.partial(inner_kernel, factors, PARTS), "inner_blocks", [VMEM] * (7 + 2 * PARTS), outs
+            functools.partial(inner_kernel, factors, PARTS),
+            "inner_blocks",
+            [VMEM] * (7 + 2 * PARTS),
+            outs,
+            [turned, turned, pltpu.SemaphoreType.DMA((2, slots))] if factors is None else [],
+            HBM if factors is None else VMEM,
         )(own, lower, upper, marks, direction, residual, *(s[2] for s in states), *(s[3] for s in states), total)
         residual, total = got[:2]
         if factors is not None:
@@ -335,14 +365,15 @@
                 for k in range(PARTS)
             ]
     (residual,) = call(
-        functools.partial(last_kernel, PARTS),
+        functools.partial(last_kernel, PARTS, slots),
         "last_residual",
-        [VMEM] * (2 + 3 * PARTS),
+        [SMEM, VMEM, HBM] + [VMEM] * (3 * PARTS),
         [(gap.shape, F32)],
-        [pltpu.VMEM((slots, h, cases), F32), pltpu.SemaphoreType.DMA((slots,))],
+        [pltpu.VMEM((h, cases), F32), pltpu.SemaphoreType.DMA],
         HBM,
-    )(marks, residual, *(s[n] for n in (0, 1) for s in states), *came)
-    return total[None, None], residual
+        aliases={2: 0},
+    )(counts, marks, residual, *(s[n] for n in (0, 1) for s in states), *came)
+    return total, residual
 
 
 def solution(mesh):

time: 53.7 us -> 53.3 us (level)
  Pallas kernels: 14.5 us -> 13.2 us
  waiting for transfers between devices: 7.46 us -> 8.3 us
    pallas_call x3, Pallas kernels: 6.05 us -> 4.63 us  [the longest x1 2.67 us: shards(): call(operator_kernel, 'block_operators', [SMEM, VMEM, VMEM, VMEM, HBM], [...]
    ppermute x1, waiting for transfers between devices: 2.86 us -> 3.86 us  [shards(): before = lax.ppermute(ends, 'sub', forward)]
  transfers between devices with their start and end apart: 23 -> 23, of which waited for: 5 -> 5; matrix products, arithmetic and copies ran while one was open for 0% -> 0% of each run, Pallas kernels for 22% -> 20%
where the time goes in v1:
time: 53.3 us; the launch traced here: 53 us
  starting transfers between devices  29.8 us (56%)
  Pallas kernels  13.2 us (25%)
  waiting for transfers between devices  8.3 us (16%)
  between operations  1.69 us (3%)
    ppermute x10, starting transfers between devices, exchange(): even = lax.ppermute(even, ('grp', 'sub'), evens)  20.9 us
    ppermute x2, starting transfers between devices, shards(): came = [lax.ppermute(state[4], 'sub', backward) for state in states]  5.29 us
    pallas_call x6, Pallas kernels, shards(): call(functools.partial(inner_kernel, factors, PARTS), 'inner_blocks', [VM...  5.05 us
    ppermute x1, waiting for transfers between devices, shards(): before = lax.ppermute(ends, 'sub', forward)  3.86 us
    ppermute x10, waiting for transfers between devices, exchange(): even = lax.ppermute(even, ('grp', 'sub'), evens)  3.47 us
    pallas_call x10, Pallas kernels, shards(): call(functools.partial(edge_kernel, factors, slots, k * width, step == IT...  3.09 us
    ppermute x1, starting transfers between devices, shards(): before = lax.ppermute(ends, 'sub', forward)  3.02 us
    pallas_call x1, Pallas kernels, shards(): call(operator_kernel, 'block_operators', [SMEM, VMEM, VMEM, VMEM, HBM], [...  2.67 us
  transfers between devices with their start and end apart: 23, of which 5 were waited for; matrix products, arithmetic and copies ran while one was open for 0% of the time, Pallas kernels for 20%

profile of v1, /device:TPU:0, one launch (start us, length us, event | category | flops | bytes accessed | tf_op | source)
XLA Modules:
  0.0 53.0 jit_solution(13937401761075961705)
XLA Ops:
  1.4 1.2 %first_ends.1 = (f32[128,256]{1,0:T(8,128)S(1)}, f32[8,8,256]{2,1,0:T(8,128)S(1)}, s32[4,256]{1,0:T(4,128)S(1)}) custom-call(s32[1,1]{1,0:T(1,128)S(6)} %copy.8.counts, f32[1,1,4,512,512]{4,3,2,1,0:T(8,128)} %operators.3, s32[1,1,4,256]{3,2,1,0:T(4,128)} %pairs.1, f32[1,1,4,256,128]{4,3,2,1,0:T(8,128)} %gap.3), custom_call_target="tpu_custom_call" | custom-call | tf_op jit(solution)/shard_map/first_ends/pallas_call | solution.py:317
  2.6 3.0 %collective-permute-start = (f32[128,256]{1,0:T(8,128)S(1)}, f32[128,256]{1,0:T(8,128)S(1)}, u32[]{:S(2)}, u32[]{:S(2)}) collective-permute-start(f32[128,256]{1,0:T(8,128)S(1)} %get-tuple-element.120.ends), channel_id=1, source_target_pairs={{0,1},{1,2},{2,3},{3,4},{4,5},{5,6},{6,7},{7,0},{8,9},{9,10},{10,1... | collective-permute-start | bytes 393224 | tf_op jit(solution)/shard_map/ppermute | solution.py:325
  5.7 2.7 %block_operators.1 = (bf16[3,512,256]{2,1,0:T(8,128)(2,1)S(1)}, bf16[3,512,256]{2,1,0:T(8,128)(2,1)S(1)}, bf16[3,512,256]{2,1,0:T(8,128)(2,1)S(1)}, bf16[1024,25...) custom-call(s32[1,1]{1,0:T(1,128)S(6)} %copy.8.counts, ...), custom_call_target="tpu_custom_call" | custom-call | tf_op jit(solution)/shard_map/block_operators/pallas_call | solution.py:326
  8.3 3.9 %collective-permute-done.before = f32[128,256]{1,0:T(8,128)S(1)} collective-permute-done((f32[128,256]{1,0:T(8,128)S(1)}, f32[128,256]{1,0:T(8,128)S(1)}, u32[]{:S(2)}, u32[]{:S(2)}) %collective-permute-start) | collective-permute-done | bytes 131104 | tf_op jit(solution)/shard_map/ppermute | solution.py:325
  12.2 0.4 first_edges.1
  12.6 0.1 collective-permute-start.3
  12.7 0.1 collective-permute-start.4
  12.8 1.9 %collective-permute-start.1 = (f32[64,256]{1,0:T(8,128)S(1)}, f32[64,256]{1,0:T(8,128)S(1)}, u32[]{:S(2)}, u32[]{:S(2)}) collective-permute-start(f32[64,256]{1,0:T(8,128)S(1)} %get-tuple-element.133.refs_4_), channel_id=1, source_target_pairs={{0,1},{1,0},{2,3},{3,2},{4,5},{5,4},{6,7},{7,6},{8,9},{9,8},{10,11... | collective-permute-start | bytes 196616 | tf_op jit(solution)/shard_map/ppermute | solution.py:313
  14.7 0.0 collective-permute-start.2
  14.7 0.7 %inner_blocks.6 = (f32[3,128,256]{2,1,0:T(8,128)S(1)}, f32[4,128,256]{2,1,0:T(8,128)S(1)}, f32[3,128,256]{2,1,0:T(8,128)S(1)}, f32[128,256]{1,0:T(8,128)S(1)}, f32[128,256]{1,0:T(8,128)S(1)}) custom-call(bf16[3,512,256]{2,1,0:T(8,128)(2,1)S(1)} %get-tuple-element.113.own, bf16[3,512,256]{2,1,0:T(8,128)(2,1)S(1)} %get-tuple-element.114.lower, ...), custom_call_target="tpu_custom_call" | custom-call | tf_op jit(solution)/shard_map/inner_blocks/pallas_call | solution.py:347
  15.4 1.8 %collective-permute-done.3.refs_6_ = f32[64,256]{1,0:T(8,128)S(1)} collective-permute-done((f32[64,256]{1,0:T(8,128)S(1)}, f32[64,256]{1,0:T(8,128)S(1)}, u32[]{:S(2)}, u32[]{:S(2)}) %collective-permute-start.3) | collective-permute-done | bytes 65568 | tf_op jit(solution)/shard_map/ppermute | solution.py:313
  17.3 0.0 collective-permute-done.4.refs_7_
  17.3 0.3 edge_blocks.11
  17.6 2.8 %collective-permute-start.7 = (f32[64,256]{1,0:T(8,128)S(1)}, f32[64,256]{1,0:T(8,128)S(1)}, u32[]{:S(2)}, u32[]{:S(2)}) collective-permute-start(f32[64,256]{1,0:T(8,128)S(1)} %get-tuple-element.155.refs_4_), channel_id=1, source_target_pairs={{0,1},{1,0},{2,3},{3,2},{4,5},{5,4},{6,7},{7,6},{8,9},{9,8},{10,11... | collective-permute-start | bytes 196616 | tf_op jit(solution)/shard_map/ppermute | solution.py:313
  20.4 0.0 collective-permute-start.8
  20.4 0.0 collective-permute-done.1.refs_6_
  20.4 0.0 collective-permute-done.2.refs_7_
  20.4 0.3 edge_blocks.10
  20.7 1.3 %collective-permute-start.5 = (f32[64,256]{1,0:T(8,128)S(1)}, f32[64,256]{1,0:T(8,128)S(1)}, u32[]{:S(2)}, u32[]{:S(2)}) collective-permute-start(f32[64,256]{1,0:T(8,128)S(1)} %get-tuple-element.150.refs_4_), channel_id=1, source_target_pairs={{0,1},{1,0},{2,3},{3,2},{4,5},{5,4},{6,7},{7,6},{8,9},{9,8},{10,11... | collective-permute-start | bytes 196616 | tf_op jit(solution)/shard_map/ppermute | solution.py:313
  22.0 0.0 collective-permute-start.6
  22.0 0.7 %inner_blocks.7 = (f32[3,128,256]{2,1,0:T(8,128)S(1)}, f32[4,128,256]{2,1,0:T(8,128)S(1)}, f32[3,128,256]{2,1,0:T(8,128)S(1)}, f32[128,256]{1,0:T(8,128)S(1)}, f32[128,256]{1,0:T(8,128)S(1)}) custom-call(bf16[3,512,256]{2,1,0:T(8,128)(2,1)S(1)} %get-tuple-element.113.own, bf16[3,512,256]{2,1,0:T(8,128)(2,1)S(1)} %get-tuple-element.114.lower, ...), custom_call_target="tpu_custom_call" | custom-call | tf_op jit(solution)/shard_map/inner_blocks/pallas_call | solution.py:347
  22.7 0.0 collective-permute-done.7.refs_6_
  22.7 0.0 collective-permute-done.8.refs_7_
  22.7 0.3 edge_blocks.13
  23.1 3.9 %collective-permute-start.11 = (f32[64,256]{1,0:T(8,128)S(1)}, f32[64,256]{1,0:T(8,128)S(1)}, u32[]{:S(2)}, u32[]{:S(2)}) collective-permute-start(f32[64,256]{1,0:T(8,128)S(1)} %get-tuple-element.172.refs_4_), channel_id=1, source_target_pairs={{0,1},{1,0},{2,3},{3,2},{4,5},{5,4},{6,7},{7,6},{8,9},{9,8},{10,11... | collective-permute-start | bytes 196616 | tf_op jit(solution)/shard_map/ppermute | solution.py:313
  27.0 0.0 collective-permute-start.12
  27.0 0.0 collective-permute-done.5.refs_6_
  27.0 0.0 collective-permute-done.6.refs_7_
  27.0 0.3 edge_blocks.12
  27.3 0.6 %collective-permute-start.10 = (f32[64,256]{1,0:T(8,128)S(1)}, f32[64,256]{1,0:T(8,128)S(1)}, u32[]{:S(2)}, u32[]{:S(2)}) collective-permute-start(f32[64,256]{1,0:T(8,128)S(1)} %get-tuple-element.168.refs_5_), channel_id=1, source_target_pairs={{0,8},{1,2},{2,1},{3,4},{4,3},{5,6},{6,5},{7,15},{8,0},{9,10},{10,... | collective-permute-start | bytes 196616 | tf_op jit(solution)/shard_map/ppermute | solution.py:312
  27.9 4.3 %collective-permute-start.9 = (f32[64,256]{1,0:T(8,128)S(1)}, f32[64,256]{1,0:T(8,128)S(1)}, u32[]{:S(2)}, u32[]{:S(2)}) collective-permute-start(f32[64,256]{1,0:T(8,128)S(1)} %get-tuple-element.167.refs_4_), channel_id=1, source_target_pairs={{0,1},{1,0},{2,3},{3,2},{4,5},{5,4},{6,7},{7,6},{8,9},{9,8},{10,11... | collective-permute-start | bytes 196616 | tf_op jit(solution)/shard_map/ppermute | solution.py:313
  32.2 0.7 %inner_blocks.8 = (f32[3,128,256]{2,1,0:T(8,128)S(1)}, f32[4,128,256]{2,1,0:T(8,128)S(1)}, f32[3,128,256]{2,1,0:T(8,128)S(1)}, f32[128,256]{1,0:T(8,128)S(1)}, f32[128,256]{1,0:T(8,128)S(1)}) custom-call(bf16[3,512,256]{2,1,0:T(8,128)(2,1)S(1)} %get-tuple-element.113.own, bf16[3,512,256]{2,1,0:T(8,128)(2,1)S(1)} %get-tuple-element.114.lower, ...), custom_call_target="tpu_custom_call" | custom-call | tf_op jit(solution)/shard_map/inner_blocks/pallas_call | solution.py:347
  32.9 0.0 collective-permute-done.11.refs_6_
  32.9 0.0 collective-permute-done.12.refs_7_
  32.9 0.3 edge_blocks.15
  33.2 0.2 collective-permute-start.15
  33.4 0.0 collective-permute-start.16
  33.4 0.0 collective-permute-done.10.refs_7_
  33.4 1.0 %collective-permute-done.9.refs_6_ = f32[64,256]{1,0:T(8,128)S(1)} collective-permute-done((f32[64,256]{1,0:T(8,128)S(1)}, f32[64,256]{1,0:T(8,128)S(1)}, u32[]{:S(2)}, u32[]{:S(2)}) %collective-permute-start.9) | collective-permute-done | bytes 65568 | tf_op jit(solution)/shard_map/ppermute | solution.py:313
  34.4 0.3 edge_blocks.14
  34.7 2.1 %collective-permute-start.13 = (f32[64,256]{1,0:T(8,128)S(1)}, f32[64,256]{1,0:T(8,128)S(1)}, u32[]{:S(2)}, u32[]{:S(2)}) collective-permute-start(f32[64,256]{1,0:T(8,128)S(1)} %get-tuple-element.184.refs_4_), channel_id=1, source_target_pairs={{0,1},{1,0},{2,3},{3,2},{4,5},{5,4},{6,7},{7,6},{8,9},{9,8},{10,11... | collective-permute-start | bytes 196616 | tf_op jit(solution)/shard_map/ppermute | solution.py:313
  36.8 0.0 collective-permute-start.14
  36.8 0.7 %inner_blocks.9 = (f32[3,128,256]{2,1,0:T(8,128)S(1)}, f32[4,128,256]{2,1,0:T(8,128)S(1)}, f32[3,128,256]{2,1,0:T(8,128)S(1)}, f32[128,256]{1,0:T(8,128)S(1)}, f32[128,256]{1,0:T(8,128)S(1)}) custom-call(bf16[3,512,256]{2,1,0:T(8,128)(2,1)S(1)} %get-tuple-element.113.own, bf16[3,512,256]{2,1,0:T(8,128)(2,1)S(1)} %get-tuple-element.114.lower, ...), custom_call_target="tpu_custom_call" | custom-call | tf_op jit(solution)/shard_map/inner_blocks/pallas_call | solution.py:347
  37.5 0.7 %collective-permute-done.15.refs_6_ = f32[64,256]{1,0:T(8,128)S(1)} collective-permute-done((f32[64,256]{1,0:T(8,128)S(1)}, f32[64,256]{1,0:T(8,128)S(1)}, u32[]{:S(2)}, u32[]{:S(2)}) %collective-permute-start.15) | collective-permute-done | bytes 65568 | tf_op jit(solution)/shard_map/ppermute | solution.py:313
  38.2 0.0 collective-permute-done.16.refs_7_
  38.2 0.3 edge_blocks.17
  38.5 2.9 %collective-permute-start.19 = (f32[64,256]{1,0:T(8,128)S(1)}, f32[64,256]{1,0:T(8,128)S(1)}, u32[]{:S(2)}, u32[]{:S(2)}) collective-permute-start(f32[64,256]{1,0:T(8,128)S(1)} %get-tuple-element.206.refs_4_), channel_id=1, source_target_pairs={{0,1},{1,0},{2,3},{3,2},{4,5},{5,4},{6,7},{7,6},{8,9},{9,8},{10,11... | collective-permute-start | bytes 196616 | tf_op jit(solution)/shard_map/ppermute | solution.py:313
  41.4 0.0 collective-permute-start.20
  41.4 0.0 collective-permute-done.13.refs_6_
  41.4 0.3 edge_blocks.16
  41.7 1.4 %collective-permute-start.17 = (f32[64,256]{1,0:T(8,128)S(1)}, f32[64,256]{1,0:T(8,128)S(1)}, u32[]{:S(2)}, u32[]{:S(2)}) collective-permute-start(f32[64,256]{1,0:T(8,128)S(1)} %get-tuple-element.201.refs_4_), channel_id=1, source_target_pairs={{0,1},{1,0},{2,3},{3,2},{4,5},{5,4},{6,7},{7,6},{8,9},{9,8},{10,11... | collective-permute-start | bytes 196616 | tf_op jit(solution)/shard_map/ppermute | solution.py:313
  43.1 0.0 collective-permute-start.18
  43.1 0.7 %inner_blocks.10 = (f32[3,128,256]{2,1,0:T(8,128)S(1)}, f32[4,128,256]{2,1,0:T(8,128)S(1)}, f32[3,128,256]{2,1,0:T(8,128)S(1)}, f32[128,256]{1,0:T(8,128)S(1)}, f32[128,256]{1,0:T(8,128)S(1)}) custom-call(bf16[3,512,256]{2,1,0:T(8,128)(2,1)S(1)} %get-tuple-element.113.own, bf16[3,512,256]{2,1,0:T(8,128)(2,1)S(1)} %get-tuple-element.114.lower, ...), custom_call_target="tpu_custom_call" | custom-call | tf_op jit(solution)/shard_map/inner_blocks/pallas_call | solution.py:347
  43.8 0.0 collective-permute-done.19.refs_6_
  43.8 0.0 collective-permute-done.20.refs_7_
  43.9 0.3 edge_blocks.19
  44.2 2.9 %collective-permute-start.22 = (f32[64,256]{1,0:T(8,128)S(1)}, f32[64,256]{1,0:T(8,128)S(1)}, u32[]{:S(2)}, u32[]{:S(2)}) collective-permute-start(f32[64,256]{1,0:T(8,128)S(1)} %get-tuple-element.219), channel_id=1, source_target_pairs={{1,0},{2,1},{3,2},{4,3},{5,4},{6,5},{7,6},{0,7},{9,8},{10,9},{11,1... | collective-permute-start | bytes 196616 | tf_op jit(solution)/shard_map/ppermute | solution.py:340
  47.1 0.0 collective-permute-done.17.refs_6_
  47.1 0.0 collective-permute-done.18.refs_7_
  47.1 0.3 edge_blocks.18
  47.4 2.4 %collective-permute-start.21 = (f32[64,256]{1,0:T(8,128)S(1)}, f32[64,256]{1,0:T(8,128)S(1)}, u32[]{:S(2)}, u32[]{:S(2)}) collective-permute-start(f32[64,256]{1,0:T(8,128)S(1)} %get-tuple-element.218), channel_id=1, source_target_pairs={{1,0},{2,1},{3,2},{4,3},{5,4},{6,5},{7,6},{0,7},{9,8},{10,9},{11,1... | collective-permute-start | bytes 196616 | tf_op jit(solution)/shard_map/ppermute | solution.py:340
  49.8 1.5 %inner_blocks.11 = (f32[1,1,4,256,128]{4,3,2,1,0:T(8,128)}, f32[1,1,4,256,128]{4,3,2,1,0:T(8,128)}) custom-call(bf16[3,512,256]{2,1,0:T(8,128)(2,1)S(1)} %get-tuple-element.113.own, bf16[3,512,256]{2,1,0:T(8,128)(2,1)S(1)} %get-tuple-element.114.lower, bf16[3,512,256]{2,1,0:T(8,128)(2,1)S(1)} %get-tuple-element.115.upper, ...), custom_call_target="tpu_custom_call" | custom-call | tf_op jit(solution)/shard_map/inner_blocks/pallas_call | solution.py:347
  51.3 0.9 %collective-permute-done.21.refs_4_ = f32[64,256]{1,0:T(8,128)S(1)} collective-permute-done((f32[64,256]{1,0:T(8,128)S(1)}, f32[64,256]{1,0:T(8,128)S(1)}, u32[]{:S(2)}, u32[]{:S(2)}) %collective-permute-start.21) | collective-permute-done | bytes 65568 | tf_op jit(solution)/shard_map/ppermute | solution.py:340
  52.3 0.8 %last_residual.1 = f32[1,1,4,256,128]{4,3,2,1,0:T(8,128)} custom-call(s32[1,1]{1,0:T(1,128)S(6)} %copy.8.counts, f32[8,8,256]{2,1,0:T(8,128)S(1)} %get-tuple-element.112.marks, f32[1,1,4,256,128]{4,3,2,1,0:T(8,128)} %get-tuple-element.213._, f32[64,256]{1,0:T(8,128)S(1)} %get-tuple-element.214.refs_0_, ...), custom_call_target="tpu_custom_call", output_to_operand_aliasing={{}: (2, {})} | custom-call | tf_op jit(solution)/shard_map/last_residual/pallas_call | solution.py:367
  (5 shorter events, 0.0 us)
Async XLA Ops:
  0.6 5.0 %copy-start = (f32[1,1,4,512,512]{4,3,2,1,0:T(8,128)S(1)}, f32[1,1,4,512,512]{4,3,2,1,0:T(8,128)}, u32[]{:S(2)}) copy-start(f32[1,1,4,512,512]{4,3,2,1,0:T(8,128)} %operators.3) | copy-start | bytes 12582916
  2.6 9.6 %collective-permute-start = (f32[128,256]{1,0:T(8,128)S(1)}, f32[128,256]{1,0:T(8,128)S(1)}, u32[]{:S(2)}, u32[]{:S(2)}) collective-permute-start(f32[128,256]{1,0:T(8,128)S(1)} %get-tuple-element.120.ends), channel_id=1, source_target_pairs={{0,1},{1,2},{2,3},{3,4},{4,5},{5,6},{6,7},{7,0},{8,9},{9,10},{10,1... | collective-permute-start | bytes 393224 | tf_op jit(solution)/shard_map/ppermute | solution.py:325
  12.6 4.7 %collective-permute-start.3 = (f32[64,256]{1,0:T(8,128)S(1)}, f32[64,256]{1,0:T(8,128)S(1)}, u32[]{:S(2)}, u32[]{:S(2)}) collective-permute-start(f32[64,256]{1,0:T(8,128)S(1)} %get-tuple-element.138.refs_4_), channel_id=1, source_target_pairs={{0,1},{1,0},{2,3},{3,2},{4,5},{5,4},{6,7},{7,6},{8,9},{9,8},{10,11... | collective-permute-start | bytes 196616 | tf_op jit(solution)/shard_map/ppermute | solution.py:313
  12.7 4.6 %collective-permute-start.4 = (f32[64,256]{1,0:T(8,128)S(1)}, f32[64,256]{1,0:T(8,128)S(1)}, u32[]{:S(2)}, u32[]{:S(2)}) collective-permute-start(f32[64,256]{1,0:T(8,128)S(1)} %get-tuple-element.139.refs_5_), channel_id=1, source_target_pairs={{0,8},{1,2},{2,1},{3,4},{4,3},{5,6},{6,5},{7,15},{8,0},{9,10},{10,... | collective-permute-start | bytes 196616 | tf_op jit(solution)/shard_map/ppermute | solution.py:312
  12.8 7.6 %collective-permute-start.1 = (f32[64,256]{1,0:T(8,128)S(1)}, f32[64,256]{1,0:T(8,128)S(1)}, u32[]{:S(2)}, u32[]{:S(2)}) collective-permute-start(f32[64,256]{1,0:T(8,128)S(1)} %get-tuple-element.133.refs_4_), channel_id=1, source_target_pairs={{0,1},{1,0},{2,3},{3,2},{4,5},{5,4},{6,7},{7,6},{8,9},{9,8},{10,11... | collective-permute-start | bytes 196616 | tf_op jit(solution)/shard_map/ppermute | solution.py:313
  14.7 5.7 %collective-permute-start.2 = (f32[64,256]{1,0:T(8,128)S(1)}, f32[64,256]{1,0:T(8,128)S(1)}, u32[]{:S(2)}, u32[]{:S(2)}) collective-permute-start(f32[64,256]{1,0:T(8,128)S(1)} %get-tuple-element.134.refs_5_), channel_id=1, source_target_pairs={{0,8},{1,2},{2,1},{3,4},{4,3},{5,6},{6,5},{7,15},{8,0},{9,10},{10,... | collective-permute-start | bytes 196616 | tf_op jit(solution)/shard_map/ppermute | solution.py:312
  17.6 5.1 %collective-permute-start.7 = (f32[64,256]{1,0:T(8,128)S(1)}, f32[64,256]{1,0:T(8,128)S(1)}, u32[]{:S(2)}, u32[]{:S(2)}) collective-permute-start(f32[64,256]{1,0:T(8,128)S(1)} %get-tuple-element.155.refs_4_), channel_id=1, source_target_pairs={{0,1},{1,0},{2,3},{3,2},{4,5},{5,4},{6,7},{7,6},{8,9},{9,8},{10,11... | collective-permute-start | bytes 196616 | tf_op jit(solution)/shard_map/ppermute | solution.py:313
  20.4 2.4 %collective-permute-start.8 = (f32[64,256]{1,0:T(8,128)S(1)}, f32[64,256]{1,0:T(8,128)S(1)}, u32[]{:S(2)}, u32[]{:S(2)}) collective-permute-start(f32[64,256]{1,0:T(8,128)S(1)} %get-tuple-element.156.refs_5_), channel_id=1, source_target_pairs={{0,8},{1,2},{2,1},{3,4},{4,3},{5,6},{6,5},{7,15},{8,0},{9,10},{10,... | collective-permute-start | bytes 196616 | tf_op jit(solution)/shard_map/ppermute | solution.py:312
  20.7 6.2 %collective-permute-start.5 = (f32[64,256]{1,0:T(8,128)S(1)}, f32[64,256]{1,0:T(8,128)S(1)}, u32[]{:S(2)}, u32[]{:S(2)}) collective-permute-start(f32[64,256]{1,0:T(8,128)S(1)} %get-tuple-element.150.refs_4_), channel_id=1, source_target_pairs={{0,1},{1,0},{2,3},{3,2},{4,5},{5,4},{6,7},{7,6},{8,9},{9,8},{10,11... | collective-permute-start | bytes 196616 | tf_op jit(solution)/shard_map/ppermute | solution.py:313
  22.0 4.9 %collective-permute-start.6 = (f32[64,256]{1,0:T(8,128)S(1)}, f32[64,256]{1,0:T(8,128)S(1)}, u32[]{:S(2)}, u32[]{:S(2)}) collective-permute-start(f32[64,256]{1,0:T(8,128)S(1)} %get-tuple-element.151.refs_5_), channel_id=1, source_target_pairs={{0,8},{1,2},{2,1},{3,4},{4,3},{5,6},{6,5},{7,15},{8,0},{9,10},{10,... | collective-permute-start | bytes 196616 | tf_op jit(solution)/shard_map/ppermute | solution.py:312
  23.1 9.8 %collective-permute-start.11 = (f32[64,256]{1,0:T(8,128)S(1)}, f32[64,256]{1,0:T(8,128)S(1)}, u32[]{:S(2)}, u32[]{:S(2)}) collective-permute-start(f32[64,256]{1,0:T(8,128)S(1)} %get-tuple-element.172.refs_4_), channel_id=1, source_target_pairs={{0,1},{1,0},{2,3},{3,2},{4,5},{5,4},{6,7},{7,6},{8,9},{9,8},{10,11... | collective-permute-start | bytes 196616 | tf_op jit(solution)/shard_map/ppermute | solution.py:313
  27.0 5.9 %collective-permute-start.12 = (f32[64,256]{1,0:T(8,128)S(1)}, f32[64,256]{1,0:T(8,128)S(1)}, u32[]{:S(2)}, u32[]{:S(2)}) collective-permute-start(f32[64,256]{1,0:T(8,128)S(1)} %get-tuple-element.173.refs_5_), channel_id=1, source_target_pairs={{0,8},{1,2},{2,1},{3,4},{4,3},{5,6},{6,5},{7,15},{8,0},{9,10},{10,... | collective-permute-start | bytes 196616 | tf_op jit(solution)/shard_map/ppermute | solution.py:312
  27.3 6.1 %collective-permute-start.10 = (f32[64,256]{1,0:T(8,128)S(1)}, f32[64,256]{1,0:T(8,128)S(1)}, u32[]{:S(2)}, u32[]{:S(2)}) collective-permute-start(f32[64,256]{1,0:T(8,128)S(1)} %get-tuple-element.168.refs_5_), channel_id=1, source_target_pairs={{0,8},{1,2},{2,1},{3,4},{4,3},{5,6},{6,5},{7,15},{8,0},{9,10},{10,... | collective-permute-start | bytes 196616 | tf_op jit(solution)/shard_map/ppermute | solution.py:312
  27.9 6.5 %collective-permute-start.9 = (f32[64,256]{1,0:T(8,128)S(1)}, f32[64,256]{1,0:T(8,128)S(1)}, u32[]{:S(2)}, u32[]{:S(2)}) collective-permute-start(f32[64,256]{1,0:T(8,128)S(1)} %get-tuple-element.167.refs_4_), channel_id=1, source_target_pairs={{0,1},{1,0},{2,3},{3,2},{4,5},{5,4},{6,7},{7,6},{8,9},{9,8},{10,11... | collective-permute-start | bytes 196616 | tf_op jit(solution)/shard_map/ppermute | solution.py:313
  33.2 5.0 %collective-permute-start.15 = (f32[64,256]{1,0:T(8,128)S(1)}, f32[64,256]{1,0:T(8,128)S(1)}, u32[]{:S(2)}, u32[]{:S(2)}) collective-permute-start(f32[64,256]{1,0:T(8,128)S(1)} %get-tuple-element.189.refs_4_), channel_id=1, source_target_pairs={{0,1},{1,0},{2,3},{3,2},{4,5},{5,4},{6,7},{7,6},{8,9},{9,8},{10,11... | collective-permute-start | bytes 196616 | tf_op jit(solution)/shard_map/ppermute | solution.py:313
  33.4 4.8 %collective-permute-start.16 = (f32[64,256]{1,0:T(8,128)S(1)}, f32[64,256]{1,0:T(8,128)S(1)}, u32[]{:S(2)}, u32[]{:S(2)}) collective-permute-start(f32[64,256]{1,0:T(8,128)S(1)} %get-tuple-element.190.refs_5_), channel_id=1, source_target_pairs={{0,8},{1,2},{2,1},{3,4},{4,3},{5,6},{6,5},{7,15},{8,0},{9,10},{10,... | collective-permute-start | bytes 196616 | tf_op jit(solution)/shard_map/ppermute | solution.py:312
  34.7 6.7 %collective-permute-start.13 = (f32[64,256]{1,0:T(8,128)S(1)}, f32[64,256]{1,0:T(8,128)S(1)}, u32[]{:S(2)}, u32[]{:S(2)}) collective-permute-start(f32[64,256]{1,0:T(8,128)S(1)} %get-tuple-element.184.refs_4_), channel_id=1, source_target_pairs={{0,1},{1,0},{2,3},{3,2},{4,5},{5,4},{6,7},{7,6},{8,9},{9,8},{10,11... | collective-permute-start | bytes 196616 | tf_op jit(solution)/shard_map/ppermute | solution.py:313
  36.8 4.6 %collective-permute-start.14 = (f32[64,256]{1,0:T(8,128)S(1)}, f32[64,256]{1,0:T(8,128)S(1)}, u32[]{:S(2)}, u32[]{:S(2)}) collective-permute-start(f32[64,256]{1,0:T(8,128)S(1)} %get-tuple-element.185.refs_5_), channel_id=1, source_target_pairs={{0,8},{1,2},{2,1},{3,4},{4,3},{5,6},{6,5},{7,15},{8,0},{9,10},{10,... | collective-permute-start | bytes 196616 | tf_op jit(solution)/shard_map/ppermute | solution.py:312
  38.5 5.3 %collective-permute-start.19 = (f32[64,256]{1,0:T(8,128)S(1)}, f32[64,256]{1,0:T(8,128)S(1)}, u32[]{:S(2)}, u32[]{:S(2)}) collective-permute-start(f32[64,256]{1,0:T(8,128)S(1)} %get-tuple-element.206.refs_4_), channel_id=1, source_target_pairs={{0,1},{1,0},{2,3},{3,2},{4,5},{5,4},{6,7},{7,6},{8,9},{9,8},{10,11... | collective-permute-start | bytes 196616 | tf_op jit(solution)/shard_map/ppermute | solution.py:313
  41.4 2.4 %collective-permute-start.20 = (f32[64,256]{1,0:T(8,128)S(1)}, f32[64,256]{1,0:T(8,128)S(1)}, u32[]{:S(2)}, u32[]{:S(2)}) collective-permute-start(f32[64,256]{1,0:T(8,128)S(1)} %get-tuple-element.207.refs_5_), channel_id=1, source_target_pairs={{0,8},{1,2},{2,1},{3,4},{4,3},{5,6},{6,5},{7,15},{8,0},{9,10},{10,... | collective-permute-start | bytes 196616 | tf_op jit(solution)/shard_map/ppermute | solution.py:312
  41.7 5.4 %collective-permute-start.17 = (f32[64,256]{1,0:T(8,128)S(1)}, f32[64,256]{1,0:T(8,128)S(1)}, u32[]{:S(2)}, u32[]{:S(2)}) collective-permute-start(f32[64,256]{1,0:T(8,128)S(1)} %get-tuple-element.201.refs_4_), channel_id=1, source_target_pairs={{0,1},{1,0},{2,3},{3,2},{4,5},{5,4},{6,7},{7,6},{8,9},{9,8},{10,11... | collective-permute-start | bytes 196616 | tf_op jit(solution)/shard_map/ppermute | solution.py:313
  43.1 4.0 %collective-permute-start.18 = (f32[64,256]{1,0:T(8,128)S(1)}, f32[64,256]{1,0:T(8,128)S(1)}, u32[]{:S(2)}, u32[]{:S(2)}) collective-permute-start(f32[64,256]{1,0:T(8,128)S(1)} %get-tuple-element.202.refs_5_), channel_id=1, source_target_pairs={{0,8},{1,2},{2,1},{3,4},{4,3},{5,6},{6,5},{7,15},{8,0},{9,10},{10,... | collective-permute-start | bytes 196616 | tf_op jit(solution)/shard_map/ppermute | solution.py:312
  44.2 7.1 %collective-permute-start.22 = (f32[64,256]{1,0:T(8,128)S(1)}, f32[64,256]{1,0:T(8,128)S(1)}, u32[]{:S(2)}, u32[]{:S(2)}) collective-permute-start(f32[64,256]{1,0:T(8,128)S(1)} %get-tuple-element.219), channel_id=1, source_target_pairs={{1,0},{2,1},{3,2},{4,3},{5,4},{6,5},{7,6},{0,7},{9,8},{10,9},{11,1... | collective-permute-start | bytes 196616 | tf_op jit(solution)/shard_map/ppermute | solution.py:340
  47.4 4.9 %collective-permute-start.21 = (f32[64,256]{1,0:T(8,128)S(1)}, f32[64,256]{1,0:T(8,128)S(1)}, u32[]{:S(2)}, u32[]{:S(2)}) collective-permute-start(f32[64,256]{1,0:T(8,128)S(1)} %get-tuple-element.218), channel_id=1, source_target_pairs={{1,0},{2,1},{3,2},{4,3},{5,4},{6,5},{7,6},{0,7},{9,8},{10,9},{11,1... | collective-permute-start | bytes 196616 | tf_op jit(solution)/shard_map/ppermute | solution.py:340

commit v2 on v1

--- a/solution.py
+++ b/solution.py
@@ -182,17 +182,17 @@
     )
 
 
-def first_edge_kernel(slots, parts, even_operator, odd_operator, marks, ends, before, beside_even, beside_odd, *outs):
+def first_edge_kernel(slots, start, even_operator, odd_operator, marks, ends, before, beside_even, beside_odd, *outs):
     place = mark_places(slots)
+    rows = pl.ds(start, outs[0].shape[0])
     is_even = row(marks, place["even"]) > 0.5
-    even = jnp.where(is_even, ends[...], before[...]) * row(marks, place["evens"])
-    odd = jnp.where(is_even, before[...], ends[...]) * row(marks, place["odds"])
+    last, first = ends[rows, :], before[rows, :]
+    even = jnp.where(is_even, last, first) * row(marks, place["evens"])
+    odd = jnp.where(is_even, first, last) * row(marks, place["odds"])
     directions = even / CENTRE, odd / CENTRE
-    given = give(marks, slots, *directions, beside_even[...], beside_odd[...], even_operator, odd_operator)
-    height = even.shape[0] // parts
-    for k in range(parts):
-        for n, x in enumerate((even, odd, *directions, *given)):
-            outs[6 * k + n][...] = x[k * height : (k + 1) * height]
+    given = give(marks, slots, *directions, beside_even[rows, :], beside_odd[rows, :], even_operator, odd_operator)
+    for out, x in zip(outs, (even, odd, *directions, *given)):
+        out[...] = x
 
 
 def edge_kernel(factors, slots, start, ends, even_operator, odd_operator, marks, beside_even, beside_odd, *refs):
@@ -330,10 +330,12 @@
         [matrices] * 3 + [pair] * 2 + [inner] * 2 + [block] * 2,
         [pltpu.VMEM((slots - 1, h, cases), F32), pltpu.SemaphoreType.DMA],
     )(counts, operators, pairs, marks, gap)
-    got = call(
-        functools.partial(first_edge_kernel, slots, PARTS), "first_edges", [VMEM] * 7, [part] * (6 * PARTS)
-    )(even_operator, odd_operator, marks, ends, before, *beside)
-    states = [got[6 * k : 6 * k + 6] for k in range(PARTS)]
+    states = [
+        call(functools.partial(first_edge_kernel, slots, k * width), "first_edges", [VMEM] * 7, [part] * 6)(
+            even_operator, odd_operator, marks, ends, before, *beside
+        )
+        for k in range(PARTS)
+    ]
     total = jnp.zeros(field[0], F32)
     for step, factors in enumerate(chebyshev_factors() + [None]):
         if factors is None:

time: 53.3 us -> 53.7 us (level)
  transfers between devices with their start and end apart: 23 -> 23, of which waited for: 5 -> 5; matrix products, arithmetic and copies ran while one was open for 0% -> 0% of each run, Pallas kernels for 20% -> 21%
where the time goes in v2:
time: 53.7 us; the launch traced here: 53.6 us
  starting transfers between devices  29.8 us (55%)
  Pallas kernels  13.4 us (25%)
  waiting for transfers between devices  8.6 us (16%)
  between operations  1.7 us (3%)
    ppermute x10, starting transfers between devices, exchange(): even = lax.ppermute(even, ('grp', 'sub'), evens)  21.1 us
    pallas_call x6, Pallas kernels, shards(): call(functools.partial(inner_kernel, factors, PARTS), 'inner_blocks', [VM...  5.07 us
    ppermute x2, starting transfers between devices, shards(): came = [lax.ppermute(state[4], 'sub', backward) for state in states]  5.04 us
    ppermute x1, waiting for transfers between devices, shards(): before = lax.ppermute(ends, 'sub', forward)  3.86 us
    ppermute x10, waiting for transfers between devices, exchange(): even = lax.ppermute(even, ('grp', 'sub'), evens)  3.3 us
    pallas_call x10, Pallas kernels, shards(): call(functools.partial(edge_kernel, factors, slots, k * width, step == IT...  3.08 us
    ppermute x1, starting transfers between devices, shards(): before = lax.ppermute(ends, 'sub', forward)  3.02 us
    pallas_call x1, Pallas kernels, shards(): call(operator_kernel, 'block_operators', [SMEM, VMEM, VMEM, VMEM, HBM], [...  2.67 us
  transfers between devices with their start and end apart: 23, of which 5 were waited for; matrix products, arithmetic and copies ran while one was open for 0% of the time, Pallas kernels for 21%

profile of v2, /device:TPU:0, one launch (start us, length us, event | category | flops | bytes accessed | tf_op | source)
XLA Modules:
  0.0 53.6 jit_solution(9632629924767195312)
XLA Ops:
  1.4 1.2 %first_ends.1 = (f32[128,256]{1,0:T(8,128)S(1)}, f32[8,8,256]{2,1,0:T(8,128)S(1)}, s32[4,256]{1,0:T(4,128)S(1)}) custom-call(s32[1,1]{1,0:T(1,128)S(6)} %copy.8.counts, f32[1,1,4,512,512]{4,3,2,1,0:T(8,128)} %operators.3, s32[1,1,4,256]{3,2,1,0:T(4,128)} %pairs.1, f32[1,1,4,256,128]{4,3,2,1,0:T(8,128)} %gap.3), custom_call_target="tpu_custom_call" | custom-call | tf_op jit(solution)/shard_map/first_ends/pallas_call | solution.py:317
  2.6 3.0 %collective-permute-start = (f32[128,256]{1,0:T(8,128)S(1)}, f32[128,256]{1,0:T(8,128)S(1)}, u32[]{:S(2)}, u32[]{:S(2)}) collective-permute-start(f32[128,256]{1,0:T(8,128)S(1)} %get-tuple-element.120.ends), channel_id=1, source_target_pairs={{0,1},{1,2},{2,3},{3,4},{4,5},{5,6},{6,7},{7,0},{8,9},{9,10},{10,1... | collective-permute-start | bytes 393224 | tf_op jit(solution)/shard_map/ppermute | solution.py:325
  5.7 2.7 %block_operators.1 = (bf16[3,512,256]{2,1,0:T(8,128)(2,1)S(1)}, bf16[3,512,256]{2,1,0:T(8,128)(2,1)S(1)}, bf16[3,512,256]{2,1,0:T(8,128)(2,1)S(1)}, bf16[1024,25...) custom-call(s32[1,1]{1,0:T(1,128)S(6)} %copy.8.counts, ...), custom_call_target="tpu_custom_call" | custom-call | tf_op jit(solution)/shard_map/block_operators/pallas_call | solution.py:326
  8.3 3.9 %collective-permute-done.before = f32[128,256]{1,0:T(8,128)S(1)} collective-permute-done((f32[128,256]{1,0:T(8,128)S(1)}, f32[128,256]{1,0:T(8,128)S(1)}, u32[]{:S(2)}, u32[]{:S(2)}) %collective-permute-start) | collective-permute-done | bytes 131104 | tf_op jit(solution)/shard_map/ppermute | solution.py:325
  12.2 0.3 first_edges.3
  12.5 0.1 collective-permute-start.3
  12.6 0.1 collective-permute-start.4
  12.7 0.3 first_edges.2
  13.0 2.0 %collective-permute-start.1 = (f32[64,256]{1,0:T(8,128)S(1)}, f32[64,256]{1,0:T(8,128)S(1)}, u32[]{:S(2)}, u32[]{:S(2)}) collective-permute-start(f32[64,256]{1,0:T(8,128)S(1)} %get-tuple-element.133.refs_4_), channel_id=1, source_target_pairs={{0,1},{1,0},{2,3},{3,2},{4,5},{5,4},{6,7},{7,6},{8,9},{9,8},{10,11... | collective-permute-start | bytes 196616 | tf_op jit(solution)/shard_map/ppermute | solution.py:313
  15.0 0.0 collective-permute-start.2
  15.0 0.7 %inner_blocks.6 = (f32[3,128,256]{2,1,0:T(8,128)S(1)}, f32[4,128,256]{2,1,0:T(8,128)S(1)}, f32[3,128,256]{2,1,0:T(8,128)S(1)}, f32[128,256]{1,0:T(8,128)S(1)}, f32[128,256]{1,0:T(8,128)S(1)}) custom-call(bf16[3,512,256]{2,1,0:T(8,128)(2,1)S(1)} %get-tuple-element.113.own, bf16[3,512,256]{2,1,0:T(8,128)(2,1)S(1)} %get-tuple-element.114.lower, ...), custom_call_target="tpu_custom_call" | custom-call | tf_op jit(solution)/shard_map/inner_blocks/pallas_call | solution.py:349
  15.7 1.8 %collective-permute-done.3.refs_6_ = f32[64,256]{1,0:T(8,128)S(1)} collective-permute-done((f32[64,256]{1,0:T(8,128)S(1)}, f32[64,256]{1,0:T(8,128)S(1)}, u32[]{:S(2)}, u32[]{:S(2)}) %collective-permute-start.3) | collective-permute-done | bytes 65568 | tf_op jit(solution)/shard_map/ppermute | solution.py:313
  17.5 0.0 collective-permute-done.4.refs_7_
  17.5 0.3 edge_blocks.11
  17.8 2.8 %collective-permute-start.7 = (f32[64,256]{1,0:T(8,128)S(1)}, f32[64,256]{1,0:T(8,128)S(1)}, u32[]{:S(2)}, u32[]{:S(2)}) collective-permute-start(f32[64,256]{1,0:T(8,128)S(1)} %get-tuple-element.155.refs_4_), channel_id=1, source_target_pairs={{0,1},{1,0},{2,3},{3,2},{4,5},{5,4},{6,7},{7,6},{8,9},{9,8},{10,11... | collective-permute-start | bytes 196616 | tf_op jit(solution)/shard_map/ppermute | solution.py:313
  20.7 0.0 collective-permute-start.8
  20.7 0.0 collective-permute-done.1.refs_6_
  20.7 0.0 collective-permute-done.2.refs_7_
  20.7 0.3 edge_blocks.10
  21.0 1.3 %collective-permute-start.5 = (f32[64,256]{1,0:T(8,128)S(1)}, f32[64,256]{1,0:T(8,128)S(1)}, u32[]{:S(2)}, u32[]{:S(2)}) collective-permute-start(f32[64,256]{1,0:T(8,128)S(1)} %get-tuple-element.150.refs_4_), channel_id=1, source_target_pairs={{0,1},{1,0},{2,3},{3,2},{4,5},{5,4},{6,7},{7,6},{8,9},{9,8},{10,11... | collective-permute-start | bytes 196616 | tf_op jit(solution)/shard_map/ppermute | solution.py:313
  22.3 0.0 collective-permute-start.6
  22.3 0.7 %inner_blocks.7 = (f32[3,128,256]{2,1,0:T(8,128)S(1)}, f32[4,128,256]{2,1,0:T(8,128)S(1)}, f32[3,128,256]{2,1,0:T(8,128)S(1)}, f32[128,256]{1,0:T(8,128)S(1)}, f32[128,256]{1,0:T(8,128)S(1)}) custom-call(bf16[3,512,256]{2,1,0:T(8,128)(2,1)S(1)} %get-tuple-element.113.own, bf16[3,512,256]{2,1,0:T(8,128)(2,1)S(1)} %get-tuple-element.114.lower, ...), custom_call_target="tpu_custom_call" | custom-call | tf_op jit(solution)/shard_map/inner_blocks/pallas_call | solution.py:349
  23.0 0.0 collective-permute-done.7.refs_6_
  23.1 0.0 collective-permute-done.8.refs_7_
  23.1 0.3 edge_blocks.13
  23.4 3.9 %collective-permute-start.11 = (f32[64,256]{1,0:T(8,128)S(1)}, f32[64,256]{1,0:T(8,128)S(1)}, u32[]{:S(2)}, u32[]{:S(2)}) collective-permute-start(f32[64,256]{1,0:T(8,128)S(1)} %get-tuple-element.172.refs_4_), channel_id=1, source_target_pairs={{0,1},{1,0},{2,3},{3,2},{4,5},{5,4},{6,7},{7,6},{8,9},{9,8},{10,11... | collective-permute-start | bytes 196616 | tf_op jit(solution)/shard_map/ppermute | solution.py:313
  27.3 0.0 collective-permute-start.12
  27.3 0.0 collective-permute-done.5.refs_6_
  27.3 0.0 collective-permute-done.6.refs_7_
  27.3 0.3 edge_blocks.12
  27.6 0.6 %collective-permute-start.10 = (f32[64,256]{1,0:T(8,128)S(1)}, f32[64,256]{1,0:T(8,128)S(1)}, u32[]{:S(2)}, u32[]{:S(2)}) collective-permute-start(f32[64,256]{1,0:T(8,128)S(1)} %get-tuple-element.168.refs_5_), channel_id=1, source_target_pairs={{0,8},{1,2},{2,1},{3,4},{4,3},{5,6},{6,5},{7,15},{8,0},{9,10},{10,... | collective-permute-start | bytes 196616 | tf_op jit(solution)/shard_map/ppermute | solution.py:312
  28.2 4.2 %collective-permute-start.9 = (f32[64,256]{1,0:T(8,128)S(1)}, f32[64,256]{1,0:T(8,128)S(1)}, u32[]{:S(2)}, u32[]{:S(2)}) collective-permute-start(f32[64,256]{1,0:T(8,128)S(1)} %get-tuple-element.167.refs_4_), channel_id=1, source_target_pairs={{0,1},{1,0},{2,3},{3,2},{4,5},{5,4},{6,7},{7,6},{8,9},{9,8},{10,11... | collective-permute-start | bytes 196616 | tf_op jit(solution)/shard_map/ppermute | solution.py:313
  32.4 0.7 %inner_blocks.8 = (f32[3,128,256]{2,1,0:T(8,128)S(1)}, f32[4,128,256]{2,1,0:T(8,128)S(1)}, f32[3,128,256]{2,1,0:T(8,128)S(1)}, f32[128,256]{1,0:T(8,128)S(1)}, f32[128,256]{1,0:T(8,128)S(1)}) custom-call(bf16[3,512,256]{2,1,0:T(8,128)(2,1)S(1)} %get-tuple-element.113.own, bf16[3,512,256]{2,1,0:T(8,128)(2,1)S(1)} %get-tuple-element.114.lower, ...), custom_call_target="tpu_custom_call" | custom-call | tf_op jit(solution)/shard_map/inner_blocks/pallas_call | solution.py:349
  33.1 0.0 collective-permute-done.11.refs_6_
  33.1 0.0 collective-permute-done.12.refs_7_
  33.1 0.3 edge_blocks.15
  33.4 0.3 collective-permute-start.15
  33.7 0.0 collective-permute-start.16
  33.7 0.0 collective-permute-done.10.refs_7_
  33.7 0.9 %collective-permute-done.9.refs_6_ = f32[64,256]{1,0:T(8,128)S(1)} collective-permute-done((f32[64,256]{1,0:T(8,128)S(1)}, f32[64,256]{1,0:T(8,128)S(1)}, u32[]{:S(2)}, u32[]{:S(2)}) %collective-permute-start.9) | collective-permute-done | bytes 65568 | tf_op jit(solution)/shard_map/ppermute | solution.py:313
  34.6 0.3 edge_blocks.14
  34.9 2.1 %collective-permute-start.13 = (f32[64,256]{1,0:T(8,128)S(1)}, f32[64,256]{1,0:T(8,128)S(1)}, u32[]{:S(2)}, u32[]{:S(2)}) collective-permute-start(f32[64,256]{1,0:T(8,128)S(1)} %get-tuple-element.184.refs_4_), channel_id=1, source_target_pairs={{0,1},{1,0},{2,3},{3,2},{4,5},{5,4},{6,7},{7,6},{8,9},{9,8},{10,11... | collective-permute-start | bytes 196616 | tf_op jit(solution)/shard_map/ppermute | solution.py:313
  37.0 0.0 collective-permute-start.14
  37.0 0.7 %inner_blocks.9 = (f32[3,128,256]{2,1,0:T(8,128)S(1)}, f32[4,128,256]{2,1,0:T(8,128)S(1)}, f32[3,128,256]{2,1,0:T(8,128)S(1)}, f32[128,256]{1,0:T(8,128)S(1)}, f32[128,256]{1,0:T(8,128)S(1)}) custom-call(bf16[3,512,256]{2,1,0:T(8,128)(2,1)S(1)} %get-tuple-element.113.own, bf16[3,512,256]{2,1,0:T(8,128)(2,1)S(1)} %get-tuple-element.114.lower, ...), custom_call_target="tpu_custom_call" | custom-call | tf_op jit(solution)/shard_map/inner_blocks/pallas_call | solution.py:349
  37.8 0.6 %collective-permute-done.15.refs_6_ = f32[64,256]{1,0:T(8,128)S(1)} collective-permute-done((f32[64,256]{1,0:T(8,128)S(1)}, f32[64,256]{1,0:T(8,128)S(1)}, u32[]{:S(2)}, u32[]{:S(2)}) %collective-permute-start.15) | collective-permute-done | bytes 65568 | tf_op jit(solution)/shard_map/ppermute | solution.py:313
  38.3 0.0 collective-permute-done.16.refs_7_
  38.3 0.3 edge_blocks.17
  38.7 3.1 %collective-permute-start.19 = (f32[64,256]{1,0:T(8,128)S(1)}, f32[64,256]{1,0:T(8,128)S(1)}, u32[]{:S(2)}, u32[]{:S(2)}) collective-permute-start(f32[64,256]{1,0:T(8,128)S(1)} %get-tuple-element.206.refs_4_), channel_id=1, source_target_pairs={{0,1},{1,0},{2,3},{3,2},{4,5},{5,4},{6,7},{7,6},{8,9},{9,8},{10,11... | collective-permute-start | bytes 196616 | tf_op jit(solution)/shard_map/ppermute | solution.py:313
  41.7 0.0 collective-permute-start.20
  41.7 0.0 collective-permute-done.13.refs_6_
  41.7 0.0 collective-permute-done.14.refs_7_
  41.7 0.3 edge_blocks.16
  42.0 1.4 %collective-permute-start.17 = (f32[64,256]{1,0:T(8,128)S(1)}, f32[64,256]{1,0:T(8,128)S(1)}, u32[]{:S(2)}, u32[]{:S(2)}) collective-permute-start(f32[64,256]{1,0:T(8,128)S(1)} %get-tuple-element.201.refs_4_), channel_id=1, source_target_pairs={{0,1},{1,0},{2,3},{3,2},{4,5},{5,4},{6,7},{7,6},{8,9},{9,8},{10,11... | collective-permute-start | bytes 196616 | tf_op jit(solution)/shard_map/ppermute | solution.py:313
  43.5 0.0 collective-permute-start.18
  43.5 0.7 %inner_blocks.10 = (f32[3,128,256]{2,1,0:T(8,128)S(1)}, f32[4,128,256]{2,1,0:T(8,128)S(1)}, f32[3,128,256]{2,1,0:T(8,128)S(1)}, f32[128,256]{1,0:T(8,128)S(1)}, f32[128,256]{1,0:T(8,128)S(1)}) custom-call(bf16[3,512,256]{2,1,0:T(8,128)(2,1)S(1)} %get-tuple-element.113.own, bf16[3,512,256]{2,1,0:T(8,128)(2,1)S(1)} %get-tuple-element.114.lower, ...), custom_call_target="tpu_custom_call" | custom-call | tf_op jit(solution)/shard_map/inner_blocks/pallas_call | solution.py:349
  44.2 0.0 collective-permute-done.20.refs_7_
  44.2 0.3 edge_blocks.19
  44.5 2.8 %collective-permute-start.22 = (f32[64,256]{1,0:T(8,128)S(1)}, f32[64,256]{1,0:T(8,128)S(1)}, u32[]{:S(2)}, u32[]{:S(2)}) collective-permute-start(f32[64,256]{1,0:T(8,128)S(1)} %get-tuple-element.219), channel_id=1, source_target_pairs={{1,0},{2,1},{3,2},{4,3},{5,4},{6,5},{7,6},{0,7},{9,8},{10,9},{11,1... | collective-permute-start | bytes 196616 | tf_op jit(solution)/shard_map/ppermute | solution.py:342
  47.3 0.3 edge_blocks.18
  47.6 2.2 %collective-permute-start.21 = (f32[64,256]{1,0:T(8,128)S(1)}, f32[64,256]{1,0:T(8,128)S(1)}, u32[]{:S(2)}, u32[]{:S(2)}) collective-permute-start(f32[64,256]{1,0:T(8,128)S(1)} %get-tuple-element.218), channel_id=1, source_target_pairs={{1,0},{2,1},{3,2},{4,3},{5,4},{6,5},{7,6},{0,7},{9,8},{10,9},{11,1... | collective-permute-start | bytes 196616 | tf_op jit(solution)/shard_map/ppermute | solution.py:342
  49.9 1.5 %inner_blocks.11 = (f32[1,1,4,256,128]{4,3,2,1,0:T(8,128)}, f32[1,1,4,256,128]{4,3,2,1,0:T(8,128)}) custom-call(bf16[3,512,256]{2,1,0:T(8,128)(2,1)S(1)} %get-tuple-element.113.own, bf16[3,512,256]{2,1,0:T(8,128)(2,1)S(1)} %get-tuple-element.114.lower, bf16[3,512,256]{2,1,0:T(8,128)(2,1)S(1)} %get-tuple-element.115.upper, ...), custom_call_target="tpu_custom_call" | custom-call | tf_op jit(solution)/shard_map/inner_blocks/pallas_call | solution.py:349
  51.4 0.0 collective-permute-done.22.refs_5_
  51.4 1.4 %collective-permute-done.21.refs_4_ = f32[64,256]{1,0:T(8,128)S(1)} collective-permute-done((f32[64,256]{1,0:T(8,128)S(1)}, f32[64,256]{1,0:T(8,128)S(1)}, u32[]{:S(2)}, u32[]{:S(2)}) %collective-permute-start.21) | collective-permute-done | bytes 65568 | tf_op jit(solution)/shard_map/ppermute | solution.py:342
  52.8 0.8 %last_residual.1 = f32[1,1,4,256,128]{4,3,2,1,0:T(8,128)} custom-call(s32[1,1]{1,0:T(1,128)S(6)} %copy.8.counts, f32[8,8,256]{2,1,0:T(8,128)S(1)} %get-tuple-element.112.marks, f32[1,1,4,256,128]{4,3,2,1,0:T(8,128)} %get-tuple-element.213._, f32[64,256]{1,0:T(8,128)S(1)} %get-tuple-element.214.refs_0_, ...), custom_call_target="tpu_custom_call", output_to_operand_aliasing={{}: (2, {})} | custom-call | tf_op jit(solution)/shard_map/last_residual/pallas_call | solution.py:369
  (6 shorter events, 0.0 us)
Async XLA Ops:
  0.6 5.0 %copy-start = (f32[1,1,4,512,512]{4,3,2,1,0:T(8,128)S(1)}, f32[1,1,4,512,512]{4,3,2,1,0:T(8,128)}, u32[]{:S(2)}) copy-start(f32[1,1,4,512,512]{4,3,2,1,0:T(8,128)} %operators.3) | copy-start | bytes 12582916
  2.6 9.6 %collective-permute-start = (f32[128,256]{1,0:T(8,128)S(1)}, f32[128,256]{1,0:T(8,128)S(1)}, u32[]{:S(2)}, u32[]{:S(2)}) collective-permute-start(f32[128,256]{1,0:T(8,128)S(1)} %get-tuple-element.120.ends), channel_id=1, source_target_pairs={{0,1},{1,2},{2,3},{3,4},{4,5},{5,6},{6,7},{7,0},{8,9},{9,10},{10,1... | collective-permute-start | bytes 393224 | tf_op jit(solution)/shard_map/ppermute | solution.py:325
  12.5 5.0 %collective-permute-start.3 = (f32[64,256]{1,0:T(8,128)S(1)}, f32[64,256]{1,0:T(8,128)S(1)}, u32[]{:S(2)}, u32[]{:S(2)}) collective-permute-start(f32[64,256]{1,0:T(8,128)S(1)} %get-tuple-element.138.refs_4_), channel_id=1, source_target_pairs={{0,1},{1,0},{2,3},{3,2},{4,5},{5,4},{6,7},{7,6},{8,9},{9,8},{10,11... | collective-permute-start | bytes 196616 | tf_op jit(solution)/shard_map/ppermute | solution.py:313
  12.6 5.0 %collective-permute-start.4 = (f32[64,256]{1,0:T(8,128)S(1)}, f32[64,256]{1,0:T(8,128)S(1)}, u32[]{:S(2)}, u32[]{:S(2)}) collective-permute-start(f32[64,256]{1,0:T(8,128)S(1)} %get-tuple-element.139.refs_5_), channel_id=1, source_target_pairs={{0,8},{1,2},{2,1},{3,4},{4,3},{5,6},{6,5},{7,15},{8,0},{9,10},{10,... | collective-permute-start | bytes 196616 | tf_op jit(solution)/shard_map/ppermute | solution.py:312
  13.0 7.7 %collective-permute-start.1 = (f32[64,256]{1,0:T(8,128)S(1)}, f32[64,256]{1,0:T(8,128)S(1)}, u32[]{:S(2)}, u32[]{:S(2)}) collective-permute-start(f32[64,256]{1,0:T(8,128)S(1)} %get-tuple-element.133.refs_4_), channel_id=1, source_target_pairs={{0,1},{1,0},{2,3},{3,2},{4,5},{5,4},{6,7},{7,6},{8,9},{9,8},{10,11... | collective-permute-start | bytes 196616 | tf_op jit(solution)/shard_map/ppermute | solution.py:313
  15.0 5.7 %collective-permute-start.2 = (f32[64,256]{1,0:T(8,128)S(1)}, f32[64,256]{1,0:T(8,128)S(1)}, u32[]{:S(2)}, u32[]{:S(2)}) collective-permute-start(f32[64,256]{1,0:T(8,128)S(1)} %get-tuple-element.134.refs_5_), channel_id=1, source_target_pairs={{0,8},{1,2},{2,1},{3,4},{4,3},{5,6},{6,5},{7,15},{8,0},{9,10},{10,... | collective-permute-start | bytes 196616 | tf_op jit(solution)/shard_map/ppermute | solution.py:312
  17.8 5.2 %collective-permute-start.7 = (f32[64,256]{1,0:T(8,128)S(1)}, f32[64,256]{1,0:T(8,128)S(1)}, u32[]{:S(2)}, u32[]{:S(2)}) collective-permute-start(f32[64,256]{1,0:T(8,128)S(1)} %get-tuple-element.155.refs_4_), channel_id=1, source_target_pairs={{0,1},{1,0},{2,3},{3,2},{4,5},{5,4},{6,7},{7,6},{8,9},{9,8},{10,11... | collective-permute-start | bytes 196616 | tf_op jit(solution)/shard_map/ppermute | solution.py:313
  20.7 2.4 %collective-permute-start.8 = (f32[64,256]{1,0:T(8,128)S(1)}, f32[64,256]{1,0:T(8,128)S(1)}, u32[]{:S(2)}, u32[]{:S(2)}) collective-permute-start(f32[64,256]{1,0:T(8,128)S(1)} %get-tuple-element.156.refs_5_), channel_id=1, source_target_pairs={{0,8},{1,2},{2,1},{3,4},{4,3},{5,6},{6,5},{7,15},{8,0},{9,10},{10,... | collective-permute-start | bytes 196616 | tf_op jit(solution)/shard_map/ppermute | solution.py:312
  21.0 6.3 %collective-permute-start.5 = (f32[64,256]{1,0:T(8,128)S(1)}, f32[64,256]{1,0:T(8,128)S(1)}, u32[]{:S(2)}, u32[]{:S(2)}) collective-permute-start(f32[64,256]{1,0:T(8,128)S(1)} %get-tuple-element.150.refs_4_), channel_id=1, source_target_pairs={{0,1},{1,0},{2,3},{3,2},{4,5},{5,4},{6,7},{7,6},{8,9},{9,8},{10,11... | collective-permute-start | bytes 196616 | tf_op jit(solution)/shard_map/ppermute | solution.py:313
  22.3 5.0 %collective-permute-start.6 = (f32[64,256]{1,0:T(8,128)S(1)}, f32[64,256]{1,0:T(8,128)S(1)}, u32[]{:S(2)}, u32[]{:S(2)}) collective-permute-start(f32[64,256]{1,0:T(8,128)S(1)} %get-tuple-element.151.refs_5_), channel_id=1, source_target_pairs={{0,8},{1,2},{2,1},{3,4},{4,3},{5,6},{6,5},{7,15},{8,0},{9,10},{10,... | collective-permute-start | bytes 196616 | tf_op jit(solution)/shard_map/ppermute | solution.py:312
  23.4 9.7 %collective-permute-start.11 = (f32[64,256]{1,0:T(8,128)S(1)}, f32[64,256]{1,0:T(8,128)S(1)}, u32[]{:S(2)}, u32[]{:S(2)}) collective-permute-start(f32[64,256]{1,0:T(8,128)S(1)} %get-tuple-element.172.refs_4_), channel_id=1, source_target_pairs={{0,1},{1,0},{2,3},{3,2},{4,5},{5,4},{6,7},{7,6},{8,9},{9,8},{10,11... | collective-permute-start | bytes 196616 | tf_op jit(solution)/shard_map/ppermute | solution.py:313
  27.3 5.9 %collective-permute-start.12 = (f32[64,256]{1,0:T(8,128)S(1)}, f32[64,256]{1,0:T(8,128)S(1)}, u32[]{:S(2)}, u32[]{:S(2)}) collective-permute-start(f32[64,256]{1,0:T(8,128)S(1)} %get-tuple-element.173.refs_5_), channel_id=1, source_target_pairs={{0,8},{1,2},{2,1},{3,4},{4,3},{5,6},{6,5},{7,15},{8,0},{9,10},{10,... | collective-permute-start | bytes 196616 | tf_op jit(solution)/shard_map/ppermute | solution.py:312
  27.6 6.1 %collective-permute-start.10 = (f32[64,256]{1,0:T(8,128)S(1)}, f32[64,256]{1,0:T(8,128)S(1)}, u32[]{:S(2)}, u32[]{:S(2)}) collective-permute-start(f32[64,256]{1,0:T(8,128)S(1)} %get-tuple-element.168.refs_5_), channel_id=1, source_target_pairs={{0,8},{1,2},{2,1},{3,4},{4,3},{5,6},{6,5},{7,15},{8,0},{9,10},{10,... | collective-permute-start | bytes 196616 | tf_op jit(solution)/shard_map/ppermute | solution.py:312
  28.2 6.5 %collective-permute-start.9 = (f32[64,256]{1,0:T(8,128)S(1)}, f32[64,256]{1,0:T(8,128)S(1)}, u32[]{:S(2)}, u32[]{:S(2)}) collective-permute-start(f32[64,256]{1,0:T(8,128)S(1)} %get-tuple-element.167.refs_4_), channel_id=1, source_target_pairs={{0,1},{1,0},{2,3},{3,2},{4,5},{5,4},{6,7},{7,6},{8,9},{9,8},{10,11... | collective-permute-start | bytes 196616 | tf_op jit(solution)/shard_map/ppermute | solution.py:313
  33.4 4.9 %collective-permute-start.15 = (f32[64,256]{1,0:T(8,128)S(1)}, f32[64,256]{1,0:T(8,128)S(1)}, u32[]{:S(2)}, u32[]{:S(2)}) collective-permute-start(f32[64,256]{1,0:T(8,128)S(1)} %get-tuple-element.189.refs_4_), channel_id=1, source_target_pairs={{0,1},{1,0},{2,3},{3,2},{4,5},{5,4},{6,7},{7,6},{8,9},{9,8},{10,11... | collective-permute-start | bytes 196616 | tf_op jit(solution)/shard_map/ppermute | solution.py:313
  33.7 4.6 %collective-permute-start.16 = (f32[64,256]{1,0:T(8,128)S(1)}, f32[64,256]{1,0:T(8,128)S(1)}, u32[]{:S(2)}, u32[]{:S(2)}) collective-permute-start(f32[64,256]{1,0:T(8,128)S(1)} %get-tuple-element.190.refs_5_), channel_id=1, source_target_pairs={{0,8},{1,2},{2,1},{3,4},{4,3},{5,6},{6,5},{7,15},{8,0},{9,10},{10,... | collective-permute-start | bytes 196616 | tf_op jit(solution)/shard_map/ppermute | solution.py:312
  34.9 6.8 %collective-permute-start.13 = (f32[64,256]{1,0:T(8,128)S(1)}, f32[64,256]{1,0:T(8,128)S(1)}, u32[]{:S(2)}, u32[]{:S(2)}) collective-permute-start(f32[64,256]{1,0:T(8,128)S(1)} %get-tuple-element.184.refs_4_), channel_id=1, source_target_pairs={{0,1},{1,0},{2,3},{3,2},{4,5},{5,4},{6,7},{7,6},{8,9},{9,8},{10,11... | collective-permute-start | bytes 196616 | tf_op jit(solution)/shard_map/ppermute | solution.py:313
  37.0 4.7 %collective-permute-start.14 = (f32[64,256]{1,0:T(8,128)S(1)}, f32[64,256]{1,0:T(8,128)S(1)}, u32[]{:S(2)}, u32[]{:S(2)}) collective-permute-start(f32[64,256]{1,0:T(8,128)S(1)} %get-tuple-element.185.refs_5_), channel_id=1, source_target_pairs={{0,8},{1,2},{2,1},{3,4},{4,3},{5,6},{6,5},{7,15},{8,0},{9,10},{10,... | collective-permute-start | bytes 196616 | tf_op jit(solution)/shard_map/ppermute | solution.py:312
  38.7 5.5 %collective-permute-start.19 = (f32[64,256]{1,0:T(8,128)S(1)}, f32[64,256]{1,0:T(8,128)S(1)}, u32[]{:S(2)}, u32[]{:S(2)}) collective-permute-start(f32[64,256]{1,0:T(8,128)S(1)} %get-tuple-element.206.refs_4_), channel_id=1, source_target_pairs={{0,1},{1,0},{2,3},{3,2},{4,5},{5,4},{6,7},{7,6},{8,9},{9,8},{10,11... | collective-permute-start | bytes 196616 | tf_op jit(solution)/shard_map/ppermute | solution.py:313
  41.7 2.5 %collective-permute-start.20 = (f32[64,256]{1,0:T(8,128)S(1)}, f32[64,256]{1,0:T(8,128)S(1)}, u32[]{:S(2)}, u32[]{:S(2)}) collective-permute-start(f32[64,256]{1,0:T(8,128)S(1)} %get-tuple-element.207.refs_5_), channel_id=1, source_target_pairs={{0,8},{1,2},{2,1},{3,4},{4,3},{5,6},{6,5},{7,15},{8,0},{9,10},{10,... | collective-permute-start | bytes 196616 | tf_op jit(solution)/shard_map/ppermute | solution.py:312
  42.0 5.3 %collective-permute-start.17 = (f32[64,256]{1,0:T(8,128)S(1)}, f32[64,256]{1,0:T(8,128)S(1)}, u32[]{:S(2)}, u32[]{:S(2)}) collective-permute-start(f32[64,256]{1,0:T(8,128)S(1)} %get-tuple-element.201.refs_4_), channel_id=1, source_target_pairs={{0,1},{1,0},{2,3},{3,2},{4,5},{5,4},{6,7},{7,6},{8,9},{9,8},{10,11... | collective-permute-start | bytes 196616 | tf_op jit(solution)/shard_map/ppermute | solution.py:313
  43.5 3.9 %collective-permute-start.18 = (f32[64,256]{1,0:T(8,128)S(1)}, f32[64,256]{1,0:T(8,128)S(1)}, u32[]{:S(2)}, u32[]{:S(2)}) collective-permute-start(f32[64,256]{1,0:T(8,128)S(1)} %get-tuple-element.202.refs_5_), channel_id=1, source_target_pairs={{0,8},{1,2},{2,1},{3,4},{4,3},{5,6},{6,5},{7,15},{8,0},{9,10},{10,... | collective-permute-start | bytes 196616 | tf_op jit(solution)/shard_map/ppermute | solution.py:312
  44.5 6.9 %collective-permute-start.22 = (f32[64,256]{1,0:T(8,128)S(1)}, f32[64,256]{1,0:T(8,128)S(1)}, u32[]{:S(2)}, u32[]{:S(2)}) collective-permute-start(f32[64,256]{1,0:T(8,128)S(1)} %get-tuple-element.219), channel_id=1, source_target_pairs={{1,0},{2,1},{3,2},{4,3},{5,4},{6,5},{7,6},{0,7},{9,8},{10,9},{11,1... | collective-permute-start | bytes 196616 | tf_op jit(solution)/shard_map/ppermute | solution.py:342
  47.6 5.2 %collective-permute-start.21 = (f32[64,256]{1,0:T(8,128)S(1)}, f32[64,256]{1,0:T(8,128)S(1)}, u32[]{:S(2)}, u32[]{:S(2)}) collective-permute-start(f32[64,256]{1,0:T(8,128)S(1)} %get-tuple-element.218), channel_id=1, source_target_pairs={{1,0},{2,1},{3,2},{4,3},{5,4},{6,5},{7,6},{0,7},{9,8},{10,9},{11,1... | collective-permute-start | bytes 196616 | tf_op jit(solution)/shard_map/ppermute | solution.py:342
